TPU v7x, 128 devices: a whole 4x4x4 slice. The times are simulated.
128 devices in a mesh: dom: 128 (over y, z, x, core).
Axes of the slice: x: 4, y: 4, z: 4, core: 2. Of those that a mesh axis runs over, the one named last changes fastest.
Arguments:
- elem_state: bfloat16 [4096, 5, 216], P('dom'), may hold values from -6 to 6
- mass_inverse: bfloat16 [4096, 216, 216], P('dom'), as said below
- jacobian: bfloat16 [4096, 216, 216], P('dom'), may hold values from -0.4375 to 0.4375
- elem_order: int32 [4096], P('dom'), may hold values from 2 to 5
- new_owner: int32 [4096], P('dom'), may hold values from 0 to 127, as said below
- neighbors: int32 [4096, 6], P('dom'), may hold values from -1 to 4095, as said below
- penalty: bfloat16 [4096, 6], P('dom'), may hold values from 0.049804688 to 0.5
- closure_in: bfloat16 [64, 5], replicated, may hold values from -2.5 to 2.5
- closure_out: bfloat16 [5, 64], replicated, may hold values from -0.75 to 0.75
Outputs:
- migrated: float32 [6144, 5, 216], P('dom')
- migrated_mass: bfloat16 [6144, 216, 216], P('dom')
- migrated_jacobian: bfloat16 [6144, 216, 216], P('dom')
Inputs may be any that keep to these rules, and one draw needn't show every extreme that they name: new_owner never falls along the elements; each element's new owner is the device that holds it before the repartition (32 elements a device, in order) or a device beside that one; at most 8 elements pass from one device to each neighbour, and each device owns between 16 and 48 elements afterwards; 8 and 48 are reached. `neighbors`: each entry is -1 or an element within 16 places of its own element along the curve; the distance 16 is reached. `mass_inverse`: each tile has a diagonal of order one and small off-diagonal entries.
All inputs are finite; a program needn't handle non-finite values.
Results may differ from a plain program's by a relative error of at most 0.01.
Values may be sent and summed in bfloat16 or wider, within the bound.
A program may use at most 128 MiB of HBM per device.

v0:
```python
import jax
import jax.numpy as jnp
from jax import lax
from jax.sharding import PartitionSpec as P

SWEEPS = 2


def padded_2(shard, sides, width):
    for axis, dim in sides:
        size, length = (lax.axis_size(axis), shard.shape[dim])
        up = [(i, (i + 1) % size) for i in range(size - 1)]
        down = [(j, i) for i, j in up]
        last = lax.slice_in_dim(shard, length - width, length, axis=dim)
        initial = lax.slice_in_dim(shard, 0, width, axis=dim)
        before = lax.ppermute(last, axis, up)
        after = lax.ppermute(initial, axis, down)
        shard = jnp.concatenate([before, shard, after], axis=dim)
    return shard


def from_behind(shard, axis, by):
    size = lax.axis_size(axis)
    pairs = [(i, i + by) for i in range(size) if 0 <= i + by < size]
    return lax.ppermute(shard, axis, pairs)


def keep_mask(order_rows, node_count):
    limit = (order_rows + 1) ** 3
    node_ids = jnp.arange(node_count, dtype=jnp.int32)
    return (node_ids[None, :] < limit[:, None]).astype(jnp.float32)[:, None, :]


def run_sweeps(
    values,
    tiles_mass,
    tiles_jac,
    order_rows,
    near_index,
    weights_face,
    closure_in,
    closure_out,
    core_start,
    core_count,
    width,
):
    retained = keep_mask(order_rows, values.shape[2])
    weights_wide = weights_face.astype(jnp.float32)[:, :, None, None]
    current = values.astype(jnp.float32)
    for sweep_idx in range(SWEEPS):
        rounded = current.astype(jnp.bfloat16)
        weighted = jnp.einsum(
            "enm,evm->evn", tiles_mass, rounded, preferred_element_type=jnp.float32
        ).astype(jnp.bfloat16)
        extended = padded_2(weighted[core_start : core_start + core_count], (("dom", 0),), width)
        padded = jnp.concatenate(
            [extended, jnp.zeros((1,) + weighted.shape[1:], jnp.bfloat16)], axis=0
        )
        beside = jnp.take(padded, near_index, axis=0, mode="clip")
        difference = beside.astype(jnp.float32) - weighted.astype(jnp.float32)[:, None]
        coupling = jnp.sum(weights_wide * difference, axis=1)
        transport = jnp.einsum(
            "enm,evn->evm", tiles_jac, weighted, preferred_element_type=jnp.float32
        )
        hidden = jnp.tanh(
            jnp.einsum("hv,evn->ehn", closure_in, rounded, preferred_element_type=jnp.float32)
        ).astype(jnp.bfloat16)
        closure = jnp.einsum("vh,ehn->evn", closure_out, hidden, preferred_element_type=jnp.float32)
        current = (current + transport + coupling + closure) * retained
    return current


def claim(owners, position, devices, moving):
    row_count = owners.shape[0]
    row_ids = jnp.arange(row_count, dtype=jnp.int32)
    owned = owners == position
    owned = owned & ((row_ids >= moving) | (position > 0))
    owned = owned & ((row_ids < row_count - moving) | (position < devices - 1))
    owned_ints = owned.astype(jnp.int32)
    leading = jnp.argmax(owned_ints)
    filled = jnp.sum(owned_ints)
    return (leading, filled)


def place(values, leading, filled):
    padded = jnp.concatenate([values, jnp.zeros_like(values)], axis=0)
    window = lax.dynamic_slice_in_dim(padded, leading, values.shape[0], 0)
    slot_ids = jnp.arange(values.shape[0], dtype=jnp.int32)
    live = (slot_ids < filled).reshape((values.shape[0],) + (1,) * (values.ndim - 1))
    return jnp.where(live, window, jnp.zeros((), values.dtype))


def neighbor_index(adjacent, position, local_count, width):
    core_anchor = position * local_count - width
    span = local_count + 2 * width
    located = jnp.clip(adjacent - core_anchor, 0, span - 1)
    return jnp.where(adjacent < 0, span, located)


def shards(
    elem_state,
    mass_inverse,
    jacobian,
    elem_order,
    new_owner,
    neighbors,
    penalty,
    closure_in,
    closure_out,
):
    local_count = elem_state.shape[0]
    moving = local_count // 4
    reach = local_count // 2
    position = lax.axis_index("dom")
    devices = lax.axis_size("dom")

    def ship_rows(start_row, offset):
        return from_behind(
            (
                elem_state[start_row : start_row + moving],
                mass_inverse[start_row : start_row + moving],
                jacobian[start_row : start_row + moving],
                penalty[start_row : start_row + moving],
            ),
            "dom",
            offset,
        )

    def ship_meta(start_row, offset):
        return from_behind(
            (
                elem_order[start_row : start_row + moving],
                new_owner[start_row : start_row + moving],
                neighbors[start_row : start_row + moving],
            ),
            "dom",
            offset,
        )

    from_left = ship_rows(local_count - moving, 1)
    from_right = ship_rows(0, -1)
    meta_left = ship_meta(local_count - moving, 1)
    meta_right = ship_meta(0, -1)
    joined_state = jnp.concatenate([from_left[0], elem_state, from_right[0]], axis=0)
    joined_mass = jnp.concatenate([from_left[1], mass_inverse, from_right[1]], axis=0)
    joined_jac = jnp.concatenate([from_left[2], jacobian, from_right[2]], axis=0)
    joined_penalty = jnp.concatenate([from_left[3], penalty, from_right[3]], axis=0)
    joined_order = jnp.concatenate([meta_left[0], elem_order, meta_right[0]], axis=0)
    owners = jnp.concatenate([meta_left[1], new_owner, meta_right[1]], axis=0)
    adjacent = jnp.concatenate([meta_left[2], neighbors, meta_right[2]], axis=0)
    leading, filled = claim(owners, position, devices, moving)
    width = reach + moving
    near_index = neighbor_index(adjacent, position, local_count, width)
    current = run_sweeps(
        joined_state,
        joined_mass,
        joined_jac,
        joined_order,
        near_index,
        joined_penalty,
        closure_in,
        closure_out,
        moving,
        local_count,
        width,
    )
    return (
        place(current, leading, filled),
        place(joined_mass, leading, filled),
        place(joined_jac, leading, filled),
    )


def solution(mesh):
    placed = (
        P("dom", None, None),
        P("dom", None, None),
        P("dom", None, None),
        P("dom"),
        P("dom"),
        P("dom", None),
        P("dom", None),
        P(),
        P(),
    )
    return jax.shard_map(
        shards,
        mesh=mesh,
        in_specs=placed,
        out_specs=(P("dom", None, None), P("dom", None, None), P("dom", None, None)),
        check_vma=False,
    )
```

profile of v0, /device:TPU:24, one launch (start us, length us, event | category | flops | bytes accessed | tf_op | source)
XLA Modules:
  0.0 144.0 jit_solution(11746820957661452209)
XLA Ops:
  0.7 1.5 %fusion.49 = (s32[8]{0:T(128)}, s32[8]{0:T(128)}) fusion(s32[32]{0:T(128)} %param.13), kind=kLoop, calls=%fused_computation.77 | loop fusion | bytes 128 | tf_op jit(solution)/shard_map/slice | solution.py:133
  2.1 1.9 %collective-permute-start = (s32[8]{0:T(128)}, s32[8]{0:T(128)}, u32[]{:S(2)}, u32[]{:S(2)}) collective-permute-start(s32[8]{0:T(128)} %get-tuple-element.31), channel_id=1, source_target_pairs={{0,1},{1,2},{2,3},{3,4},{4,5},{5,6},{6,7},{7,8},{8,9},{9,10},{10,1... | collective-permute-start | bytes 104 | tf_op jit(solution)/shard_map/ppermute | solution.py:25
  4.1 7.9 %collective-permute-start.1 = (s32[8]{0:T(128)}, s32[8]{0:T(128)}, u32[]{:S(2)}, u32[]{:S(2)}) collective-permute-start(s32[8]{0:T(128)} %get-tuple-element.32), channel_id=1, source_target_pairs={{1,0},{2,1},{3,2},{4,3},{5,4},{6,5},{7,6},{8,7},{9,8},{10,9},{11,1... | collective-permute-start | bytes 104 | tf_op jit(solution)/shard_map/ppermute | solution.py:25
  11.9 1.3 fusion.48
  13.2 1.9 %collective-permute-start.14 = (s32[8]{0:T(128)}, s32[8]{0:T(128)}, u32[]{:S(2)}, u32[]{:S(2)}) collective-permute-start(s32[8]{0:T(128)} %get-tuple-element.29), channel_id=1, source_target_pairs={{0,1},{1,2},{2,3},{3,4},{4,5},{5,6},{6,7},{7,8},{8,9},{9,10},{10,1... | collective-permute-start | bytes 104 | tf_op jit(solution)/shard_map/ppermute | solution.py:25
  15.2 7.9 %collective-permute-start.15 = (s32[8]{0:T(128)}, s32[8]{0:T(128)}, u32[]{:S(2)}, u32[]{:S(2)}) collective-permute-start(s32[8]{0:T(128)} %get-tuple-element.30), channel_id=1, source_target_pairs={{1,0},{2,1},{3,2},{4,3},{5,4},{6,5},{7,6},{8,7},{9,8},{10,9},{11,1... | collective-permute-start | bytes 104 | tf_op jit(solution)/shard_map/ppermute | solution.py:25
  23.0 1.4 fusion.47
  24.5 1.9 %collective-permute-start.8 = (bf16[8,6]{0,1:T(8,128)(2,1)}, bf16[8,6]{0,1:T(8,128)(2,1)}, u32[]{:S(2)}, u32[]{:S(2)}) collective-permute-start(bf16[8,6]{0,1:T(8,128)(2,1)} %get-tuple-element.27), channel_id=1, source_target_pairs={{0,1},{1,2},{2,3},{3,4},{4,5},{5,6},{6,7},{7,8},{8,9},{9,10},{10,1... | collective-permute-start | bytes 296 | tf_op jit(solution)/shard_map/ppermute | solution.py:25
  26.4 1.4 fusion.46
  27.8 1.3 copy.31
  31.8 2.7 %fusion.42 = (bf16[8,216,216]{2,1,0:T(8,128)(2,1)}, bf16[8,216,216]{2,1,0:T(8,128)(2,1)}) fusion(bf16[32,216,216]{2,1,0:T(8,128)(2,1)} %param.10), kind=kLoop, calls=%fused_computation.70 | loop fusion | bytes 2985984 | tf_op jit(solution)/shard_map/slice | solution.py:121
  34.6 2.8 %fusion.41 = (bf16[8,216,216]{2,1,0:T(8,128)(2,1)}, bf16[8,216,216]{2,1,0:T(8,128)(2,1)}) fusion(bf16[32,216,216]{2,1,0:T(8,128)(2,1)} %param.11), kind=kLoop, calls=%fused_computation.69 | loop fusion | bytes 2985984 | tf_op jit(solution)/shard_map/slice | solution.py:122
  38.0 7.9 %collective-permute-start.9 = (bf16[8,6]{0,1:T(8,128)(2,1)}, bf16[8,6]{0,1:T(8,128)(2,1)}, u32[]{:S(2)}, u32[]{:S(2)}) collective-permute-start(bf16[8,6]{0,1:T(8,128)(2,1)} %get-tuple-element.28), channel_id=1, source_target_pairs={{1,0},{2,1},{3,2},{4,3},{5,4},{6,5},{7,6},{8,7},{9,8},{10,9},{11,1... | collective-permute-start | bytes 296 | tf_op jit(solution)/shard_map/ppermute | solution.py:25
  45.9 1.9 %collective-permute-start.13 = (s32[8,6]{1,0:T(8,128)}, s32[8,6]{1,0:T(8,128)}, u32[]{:S(2)}, u32[]{:S(2)}) collective-permute-start(s32[8,6]{1,0:T(8,128)} %copy.32), channel_id=1, source_target_pairs={{1,0},{2,1},{3,2},{4,3},{5,4},{6,5},{7,6},{8,7},{9,8},{10,9},{11,1... | collective-permute-start | bytes 584 | tf_op jit(solution)/shard_map/ppermute | solution.py:25
  47.8 1.5 %fusion.40 = (s32[]{:T(128)}, s32[48]{0:T(128)S(1)}) fusion(pred[]{:T(512)S(6)} %lt.62, pred[]{:T(512)S(6)} %gt.5, s32[]{:T(128)S(6)} %axis_index.12, s32[8]{0:T(128)} %collective-permute-done.1, s32[32]{0:T(128)} %param.13, s32[8]{0:T(128)} %collective-permute-done), kind=kLoop, calls=%fused_computation.68 | loop fusion | flops 527 | bytes 394 | tf_op jit(solution)/shard_map/reduce_sum | solution.py:81
  49.3 1.2 iota_compare_fusion.1
  52.4 2.4 %collective-permute-start.12 = (s32[8,6]{1,0:T(8,128)}, s32[8,6]{1,0:T(8,128)}, u32[]{:S(2)}, u32[]{:S(2)}) collective-permute-start(s32[8,6]{1,0:T(8,128)} %copy.31), channel_id=1, source_target_pairs={{0,1},{1,2},{2,3},{3,4},{4,5},{5,6},{6,7},{7,8},{8,9},{9,10},{10,1... | collective-permute-start | bytes 584 | tf_op jit(solution)/shard_map/ppermute | solution.py:25
  54.8 1.9 %collective-permute-start.2 = (bf16[8,5,216]{2,1,0:T(8,128)(2,1)}, bf16[8,5,216]{2,1,0:T(8,128)(2,1)}, u32[]{:S(2)}, u32[]{:S(2)}) collective-permute-start(bf16[8,5,216]{2,1,0:T(8,128)(2,1)} %copy.34), channel_id=1, source_target_pairs={{0,1},{1,2},{2,3},{3,4},{4,5},{5,6},{6,7},{7,8},{8,9},{9,10},{10,1... | collective-permute-start | bytes 51848 | tf_op jit(solution)/shard_map/ppermute | solution.py:25
  58.9 7.9 %collective-permute-start.3 = (bf16[8,5,216]{2,1,0:T(8,128)(2,1)}, bf16[8,5,216]{2,1,0:T(8,128)(2,1)}, u32[]{:S(2)}, u32[]{:S(2)}) collective-permute-start(bf16[8,5,216]{2,1,0:T(8,128)(2,1)} %copy.35), channel_id=1, source_target_pairs={{1,0},{2,1},{3,2},{4,3},{5,4},{6,5},{7,6},{8,7},{9,8},{10,9},{11,1... | collective-permute-start | bytes 51848 | tf_op jit(solution)/shard_map/ppermute | solution.py:25
  66.7 1.9 %collective-permute-start.4 = (bf16[8,216,216]{2,1,0:T(8,128)(2,1)}, bf16[8,216,216]{2,1,0:T(8,128)(2,1)}, u32[]{:S(2)}, u32[]{:S(2)}) collective-permute-start(bf16[8,216,216]{2,1,0:T(8,128)(2,1)} %get-tuple-element.18), channel_id=1, source_target_pairs={{0,1},{1,2},{2,3},{3,4},{4,5},{5,6},{6,7},{7,8},{8,9},{9,10},{10,1... | collective-permute-start | bytes 2239496 | tf_op jit(solution)/shard_map/ppermute | solution.py:25
  68.7 0.8 maximum_convert_fusion
  70.1 7.9 %collective-permute-start.5 = (bf16[8,216,216]{2,1,0:T(8,128)(2,1)}, bf16[8,216,216]{2,1,0:T(8,128)(2,1)}, u32[]{:S(2)}, u32[]{:S(2)}) collective-permute-start(bf16[8,216,216]{2,1,0:T(8,128)(2,1)} %get-tuple-element.17), channel_id=1, source_target_pairs={{1,0},{2,1},{3,2},{4,3},{5,4},{6,5},{7,6},{8,7},{9,8},{10,9},{11,1... | collective-permute-start | bytes 2239496 | tf_op jit(solution)/shard_map/ppermute | solution.py:25
  78.0 0.8 copy.28
  78.8 1.9 %collective-permute-start.7 = (bf16[8,216,216]{2,1,0:T(8,128)(2,1)}, bf16[8,216,216]{2,1,0:T(8,128)(2,1)}, u32[]{:S(2)}, u32[]{:S(2)}) collective-permute-start(bf16[8,216,216]{2,1,0:T(8,128)(2,1)} %get-tuple-element.15), channel_id=1, source_target_pairs={{1,0},{2,1},{3,2},{4,3},{5,4},{6,5},{7,6},{8,7},{9,8},{10,9},{11,1... | collective-permute-start | bytes 2239496 | tf_op jit(solution)/shard_map/ppermute | solution.py:25
  80.7 1.3 copy.27
  83.5 0.9 reshape.168
  84.3 2.4 %collective-permute-start.6 = (bf16[8,216,216]{2,1,0:T(8,128)(2,1)}, bf16[8,216,216]{2,1,0:T(8,128)(2,1)S(1)}, u32[]{:S(2)}, u32[]{:S(2)}) collective-permute-start(bf16[8,216,216]{2,1,0:T(8,128)(2,1)} %get-tuple-element.16), channel_id=1, source_target_pairs={{0,1},{1,2},{2,3},{3,4},{4,5},{5,6},{6,7},{7,8},{8,9},{9,10},{10,1... | collective-permute-start | bytes 2239496 | tf_op jit(solution)/shard_map/ppermute | solution.py:25
  86.8 0.8 constant_dynamic-update-slice_fusion.2
  87.5 0.9 constant_dynamic-update-slice_fusion.1
  88.5 0.8 constant_dynamic-update-slice_fusion
  89.2 1.3 constant_dynamic-update-slice_fusion.5
  90.8 1.4 constant_dynamic-update-slice_fusion.3
  92.2 2.4 %fusion.50 = (f32[48,5,216]{2,1,0:T(8,128)}, bf16[48,5,216]{2,1,0:T(8,128)(2,1)S(1)}) fusion(bf16[48,5,216]{2,1,0:T(8,128)(2,1)S(1)} %constant_dynamic-update-slice_fusion, bf16[48,216,216]{2,1,0:T(8,128)(2,1)S(1)} %constant_dynamic-update-slice_fusion.3), kind=kOutput, calls=%fused_computation.78 | convolution fusion | flops 22498560 | bytes 4893696 | tf_op jit(solution)/shard_map/enm,evm->evn/dot_general | solution.py:52
  94.6 1.9 %collective-permute-start.10 = (bf16[24,5,216]{2,1,0:T(8,128)(2,1)S(1)}, bf16[24,5,216]{2,1,0:T(8,128)(2,1)S(1)}, u32[]{:S(2)}, u32[]{:S(2)}) collective-permute-start(bf16[24,5,216]{2,1,0:T(8,128)(2,1)S(1)} %get-tuple-element.21), channel_id=1, source_target_pairs={{0,1},{1,2},{2,3},{3,4},{4,5},{5,6},{6,7},{7,8},{8,9},{9,10},{10,1... | collective-permute-start | bytes 155528 | tf_op jit(solution)/shard_map/ppermute | solution.py:16
  96.6 7.9 %collective-permute-start.11 = (bf16[24,5,216]{2,1,0:T(8,128)(2,1)S(1)}, bf16[24,5,216]{2,1,0:T(8,128)(2,1)S(1)}, u32[]{:S(2)}, u32[]{:S(2)}) collective-permute-start(bf16[24,5,216]{2,1,0:T(8,128)(2,1)S(1)} %get-tuple-element.22), channel_id=1, source_target_pairs={{1,0},{2,1},{3,2},{4,3},{5,4},{6,5},{7,6},{8,7},{9,8},{10,9},{11,1... | collective-permute-start | bytes 155528 | tf_op jit(solution)/shard_map/ppermute | solution.py:17
  104.8 1.2 constant_dynamic-update-slice_fusion.6
  106.4 10.1 %fusion.3 = (bf16[48,216,216]{2,1,0:T(8,128)(2,1)}, bf16[48,216,216]{2,1,0:T(8,128)(2,1)}) fusion(bf16[48,216,216]{2,1,0:T(8,128)(2,1)S(1)} %broadcast.64, s32[]{:T(128)S(6)} %select_n.32, bf16[8,216,216]{2,1,0:T(8,128)(2,1)S(1)} %collective-permute-done.6, bf16[32,216,216]{2,1,0:T(8,128)(2,1)S(1)} %copy-done.4, ...), kind=kLoop, calls=%fused_computation.12 | loop fusion | flops 17915904 | bytes 22394932 | tf_op jit(solution)/shard_map/jit(_where)/select_n | solution.py:90
  116.6 0.8 fusion.52
  117.7 1.8 %gather_fusion = bf16[288,5,216]{2,1,0:T(8,128)(2,1)S(1)} fusion(bf16[81,5,216]{2,1,0:T(8,128)(2,1)S(1)} %maximum_maximum_fusion, s32[1024]{0:T(1024)S(1)} %pad_clamp_fusion), kind=kCustom, calls=%fused_computation | custom fusion | bytes 1245312 | tf_op jit(solution)/shard_map/jit(_take)/gather | solution.py:59
  120.2 0.8 add_multiply_fusion
  121.1 4.0 %fusion.51 = (f32[48,5,216]{2,1,0:T(8,128)S(1)}, bf16[48,5,216]{2,1,0:T(8,128)(2,1)S(1)}) fusion(bf16[48,216,216]{2,1,0:T(8,128)(2,1)} %copy-done.1, f32[48,5,216]{2,1,0:T(8,128)S(1)} %add_multiply_fusion), kind=kOutput, calls=%fused_computation.79 | convolution fusion | flops 22550400 | bytes 4997376 | tf_op jit(solution)/shard_map/enm,evm->evn/dot_general | solution.py:52
  125.1 1.9 %collective-permute-start.16 = (bf16[24,5,216]{2,1,0:T(8,128)(2,1)S(1)}, bf16[24,5,216]{2,1,0:T(8,128)(2,1)S(1)}, u32[]{:S(2)}, u32[]{:S(2)}) collective-permute-start(bf16[24,5,216]{2,1,0:T(8,128)(2,1)S(1)} %get-tuple-element.19), channel_id=1, source_target_pairs={{0,1},{1,2},{2,3},{3,4},{4,5},{5,6},{6,7},{7,8},{8,9},{9,10},{10,1... | collective-permute-start | bytes 155528 | tf_op jit(solution)/shard_map/ppermute | solution.py:16
  127.0 8.0 %collective-permute-start.17 = (bf16[24,5,216]{2,1,0:T(8,128)(2,1)S(1)}, bf16[24,5,216]{2,1,0:T(8,128)(2,1)S(1)}, u32[]{:S(2)}, u32[]{:S(2)}) collective-permute-start(bf16[24,5,216]{2,1,0:T(8,128)(2,1)S(1)} %get-tuple-element.20), channel_id=1, source_target_pairs={{1,0},{2,1},{3,2},{4,3},{5,4},{6,5},{7,6},{8,7},{9,8},{10,9},{11,1... | collective-permute-start | bytes 155528 | tf_op jit(solution)/shard_map/ppermute | solution.py:17
  135.1 0.8 fusion.19
  135.9 1.2 collective-permute-done.17
  137.2 1.8 %gather_fusion.1 = bf16[288,5,216]{2,1,0:T(8,128)(2,1)S(1)} fusion(bf16[81,5,216]{2,1,0:T(8,128)(2,1)S(1)} %maximum_maximum_fusion.1, s32[1024]{0:T(1024)S(1)} %pad_clamp_fusion), kind=kCustom, calls=%fused_computation.1 | custom fusion | bytes 1245312 | tf_op jit(solution)/shard_map/jit(_take)/gather | solution.py:59
  139.7 3.3 %fusion.24 = f32[48,5,216]{2,1,0:T(8,128)S(1)} fusion(f32[48,5,216]{2,1,0:T(8,128)S(1)} %fusion.19, f32[48,5,216]{2,1,0:T(8,128)S(1)} %fusion.9, f32[48,5,216]{2,1,0:T(8,128)S(1)} %add_multiply_fusion, bf16[48,5,216]{2,1,0:T(8,128)(2,1)S(1)} %get-tuple-element.36, bf16[48,216,216]{2,1,0:T(8,128)(2,1)} %copy-done.2, f32[48,216]{1,0:T(8,128)S(1)} %copy-done.9), kind=kOutput, calls=%fused_computation.34 | convolution fusion | flops 22602240 | bytes 5453568 | tf_op jit(solution)/shard_map/enm,evn->evm/dot_general | solution.py:62
  143.2 0.8 copy.30
  (74 shorter events, 10.4 us)
Async XLA Ops:
  0.6 119.6 %copy-start = (bf16[5,64]{1,0:T(8,128)(2,1)S(1)}, bf16[5,64]{1,0:T(8,128)(2,1)}, u32[]{:S(2)}) copy-start(bf16[5,64]{1,0:T(8,128)(2,1)} %param.17) | copy-start | bytes 1924
  0.6 68.0 %copy-start.11 = (bf16[32,6]{0,1:T(8,128)(2,1)S(1)}, bf16[32,6]{0,1:T(8,128)(2,1)}, u32[]{:S(2)}) copy-start(bf16[32,6]{0,1:T(8,128)(2,1)} %param.15) | copy-start | bytes 1156
  0.7 81.4 %copy-start.10 = (s32[32,6]{0,1:T(8,128)S(1)}, s32[32,6]{0,1:T(8,128)}, u32[]{:S(2)}) copy-start(s32[32,6]{0,1:T(8,128)} %param.14) | copy-start | bytes 2308
  0.7 89.9 %copy-start.3 = (bf16[32,216,216]{2,1,0:T(8,128)(2,1)S(1)}, bf16[32,216,216]{2,1,0:T(8,128)(2,1)}, u32[]{:S(2)}) copy-start(bf16[32,216,216]{2,1,0:T(8,128)(2,1)} %param.10) | copy-start | bytes 8957956
  2.1 35.9 %collective-permute-start = (s32[8]{0:T(128)}, s32[8]{0:T(128)}, u32[]{:S(2)}, u32[]{:S(2)}) collective-permute-start(s32[8]{0:T(128)} %get-tuple-element.31), channel_id=1, source_target_pairs={{0,1},{1,2},{2,3},{3,4},{4,5},{5,6},{6,7},{7,8},{8,9},{9,10},{10,1... | collective-permute-start | bytes 104 | tf_op jit(solution)/shard_map/ppermute | solution.py:25
  4.1 41.8 %collective-permute-start.1 = (s32[8]{0:T(128)}, s32[8]{0:T(128)}, u32[]{:S(2)}, u32[]{:S(2)}) collective-permute-start(s32[8]{0:T(128)} %get-tuple-element.32), channel_id=1, source_target_pairs={{1,0},{2,1},{3,2},{4,3},{5,4},{6,5},{7,6},{8,7},{9,8},{10,9},{11,1... | collective-permute-start | bytes 104 | tf_op jit(solution)/shard_map/ppermute | solution.py:25
  13.2 39.1 %collective-permute-start.14 = (s32[8]{0:T(128)}, s32[8]{0:T(128)}, u32[]{:S(2)}, u32[]{:S(2)}) collective-permute-start(s32[8]{0:T(128)} %get-tuple-element.29), channel_id=1, source_target_pairs={{0,1},{1,2},{2,3},{3,4},{4,5},{5,6},{6,7},{7,8},{8,9},{9,10},{10,1... | collective-permute-start | bytes 104 | tf_op jit(solution)/shard_map/ppermute | solution.py:25
  15.2 39.7 %collective-permute-start.15 = (s32[8]{0:T(128)}, s32[8]{0:T(128)}, u32[]{:S(2)}, u32[]{:S(2)}) collective-permute-start(s32[8]{0:T(128)} %get-tuple-element.30), channel_id=1, source_target_pairs={{1,0},{2,1},{3,2},{4,3},{5,4},{6,5},{7,6},{8,7},{9,8},{10,9},{11,1... | collective-permute-start | bytes 104 | tf_op jit(solution)/shard_map/ppermute | solution.py:25
  24.5 34.4 %collective-permute-start.8 = (bf16[8,6]{0,1:T(8,128)(2,1)}, bf16[8,6]{0,1:T(8,128)(2,1)}, u32[]{:S(2)}, u32[]{:S(2)}) collective-permute-start(bf16[8,6]{0,1:T(8,128)(2,1)} %get-tuple-element.27), channel_id=1, source_target_pairs={{0,1},{1,2},{2,3},{3,4},{4,5},{5,6},{6,7},{7,8},{8,9},{9,10},{10,1... | collective-permute-start | bytes 296 | tf_op jit(solution)/shard_map/ppermute | solution.py:25
  29.8 26.9 %copy-start.12 = (s32[32]{0:T(128)S(1)}, s32[32]{0:T(128)}, u32[]{:S(2)}) copy-start(s32[32]{0:T(128)} %param.12) | copy-start | bytes 388
  38.0 28.7 %collective-permute-start.9 = (bf16[8,6]{0,1:T(8,128)(2,1)}, bf16[8,6]{0,1:T(8,128)(2,1)}, u32[]{:S(2)}, u32[]{:S(2)}) collective-permute-start(bf16[8,6]{0,1:T(8,128)(2,1)} %get-tuple-element.28), channel_id=1, source_target_pairs={{1,0},{2,1},{3,2},{4,3},{5,4},{6,5},{7,6},{8,7},{9,8},{10,9},{11,1... | collective-permute-start | bytes 296 | tf_op jit(solution)/shard_map/ppermute | solution.py:25
  45.9 24.3 %collective-permute-start.13 = (s32[8,6]{1,0:T(8,128)}, s32[8,6]{1,0:T(8,128)}, u32[]{:S(2)}, u32[]{:S(2)}) collective-permute-start(s32[8,6]{1,0:T(8,128)} %copy.32), channel_id=1, source_target_pairs={{1,0},{2,1},{3,2},{4,3},{5,4},{6,5},{7,6},{8,7},{9,8},{10,9},{11,1... | collective-permute-start | bytes 584 | tf_op jit(solution)/shard_map/ppermute | solution.py:25
  52.4 26.4 %collective-permute-start.12 = (s32[8,6]{1,0:T(8,128)}, s32[8,6]{1,0:T(8,128)}, u32[]{:S(2)}, u32[]{:S(2)}) collective-permute-start(s32[8,6]{1,0:T(8,128)} %copy.31), channel_id=1, source_target_pairs={{0,1},{1,2},{2,3},{3,4},{4,5},{5,6},{6,7},{7,8},{8,9},{9,10},{10,1... | collective-permute-start | bytes 584 | tf_op jit(solution)/shard_map/ppermute | solution.py:25
  54.8 29.5 %collective-permute-start.2 = (bf16[8,5,216]{2,1,0:T(8,128)(2,1)}, bf16[8,5,216]{2,1,0:T(8,128)(2,1)}, u32[]{:S(2)}, u32[]{:S(2)}) collective-permute-start(bf16[8,5,216]{2,1,0:T(8,128)(2,1)} %copy.34), channel_id=1, source_target_pairs={{0,1},{1,2},{2,3},{3,4},{4,5},{5,6},{6,7},{7,8},{8,9},{9,10},{10,1... | collective-permute-start | bytes 51848 | tf_op jit(solution)/shard_map/ppermute | solution.py:25
  58.9 29.6 %collective-permute-start.3 = (bf16[8,5,216]{2,1,0:T(8,128)(2,1)}, bf16[8,5,216]{2,1,0:T(8,128)(2,1)}, u32[]{:S(2)}, u32[]{:S(2)}) collective-permute-start(bf16[8,5,216]{2,1,0:T(8,128)(2,1)} %copy.35), channel_id=1, source_target_pairs={{1,0},{2,1},{3,2},{4,3},{5,4},{6,5},{7,6},{8,7},{9,8},{10,9},{11,1... | collective-permute-start | bytes 51848 | tf_op jit(solution)/shard_map/ppermute | solution.py:25
  66.7 22.5 %collective-permute-start.4 = (bf16[8,216,216]{2,1,0:T(8,128)(2,1)}, bf16[8,216,216]{2,1,0:T(8,128)(2,1)}, u32[]{:S(2)}, u32[]{:S(2)}) collective-permute-start(bf16[8,216,216]{2,1,0:T(8,128)(2,1)} %get-tuple-element.18), channel_id=1, source_target_pairs={{0,1},{1,2},{2,3},{3,4},{4,5},{5,6},{6,7},{7,8},{8,9},{9,10},{10,1... | collective-permute-start | bytes 2239496 | tf_op jit(solution)/shard_map/ppermute | solution.py:25
  70.1 20.7 %collective-permute-start.5 = (bf16[8,216,216]{2,1,0:T(8,128)(2,1)}, bf16[8,216,216]{2,1,0:T(8,128)(2,1)}, u32[]{:S(2)}, u32[]{:S(2)}) collective-permute-start(bf16[8,216,216]{2,1,0:T(8,128)(2,1)} %get-tuple-element.17), channel_id=1, source_target_pairs={{1,0},{2,1},{3,2},{4,3},{5,4},{6,5},{7,6},{8,7},{9,8},{10,9},{11,1... | collective-permute-start | bytes 2239496 | tf_op jit(solution)/shard_map/ppermute | solution.py:25
  78.8 26.0 %collective-permute-start.7 = (bf16[8,216,216]{2,1,0:T(8,128)(2,1)}, bf16[8,216,216]{2,1,0:T(8,128)(2,1)}, u32[]{:S(2)}, u32[]{:S(2)}) collective-permute-start(bf16[8,216,216]{2,1,0:T(8,128)(2,1)} %get-tuple-element.15), channel_id=1, source_target_pairs={{1,0},{2,1},{3,2},{4,3},{5,4},{6,5},{7,6},{8,7},{9,8},{10,9},{11,1... | collective-permute-start | bytes 2239496 | tf_op jit(solution)/shard_map/ppermute | solution.py:25
  84.3 20.1 %collective-permute-start.6 = (bf16[8,216,216]{2,1,0:T(8,128)(2,1)}, bf16[8,216,216]{2,1,0:T(8,128)(2,1)S(1)}, u32[]{:S(2)}, u32[]{:S(2)}) collective-permute-start(bf16[8,216,216]{2,1,0:T(8,128)(2,1)} %get-tuple-element.16), channel_id=1, source_target_pairs={{0,1},{1,2},{2,3},{3,4},{4,5},{5,6},{6,7},{7,8},{8,9},{9,10},{10,1... | collective-permute-start | bytes 2239496 | tf_op jit(solution)/shard_map/ppermute | solution.py:25
  89.2 3.0 %copy-start.6 = (bf16[48,5,216]{2,1,0:T(8,128)(2,1)}, bf16[48,5,216]{2,1,0:T(8,128)(2,1)S(1)}, u32[]{:S(2)}) copy-start(bf16[48,5,216]{2,1,0:T(8,128)(2,1)S(1)} %constant_dynamic-update-slice_fusion) | copy-start | bytes 311044
  90.8 13.7 %copy-start.4 = (bf16[32,216,216]{2,1,0:T(8,128)(2,1)S(1)}, bf16[32,216,216]{2,1,0:T(8,128)(2,1)}, u32[]{:S(2)}) copy-start(bf16[32,216,216]{2,1,0:T(8,128)(2,1)} %param.11) | copy-start | bytes 8957956
  92.2 12.6 %copy-start.1 = (bf16[48,216,216]{2,1,0:T(8,128)(2,1)}, bf16[48,216,216]{2,1,0:T(8,128)(2,1)S(1)}, u32[]{:S(2)}) copy-start(bf16[48,216,216]{2,1,0:T(8,128)(2,1)S(1)} %constant_dynamic-update-slice_fusion.3) | copy-start | bytes 13436932
  94.6 22.8 %collective-permute-start.10 = (bf16[24,5,216]{2,1,0:T(8,128)(2,1)S(1)}, bf16[24,5,216]{2,1,0:T(8,128)(2,1)S(1)}, u32[]{:S(2)}, u32[]{:S(2)}) collective-permute-start(bf16[24,5,216]{2,1,0:T(8,128)(2,1)S(1)} %get-tuple-element.21), channel_id=1, source_target_pairs={{0,1},{1,2},{2,3},{3,4},{4,5},{5,6},{6,7},{7,8},{8,9},{9,10},{10,1... | collective-permute-start | bytes 155528 | tf_op jit(solution)/shard_map/ppermute | solution.py:16
  96.6 20.9 %collective-permute-start.11 = (bf16[24,5,216]{2,1,0:T(8,128)(2,1)S(1)}, bf16[24,5,216]{2,1,0:T(8,128)(2,1)S(1)}, u32[]{:S(2)}, u32[]{:S(2)}) collective-permute-start(bf16[24,5,216]{2,1,0:T(8,128)(2,1)S(1)} %get-tuple-element.22), channel_id=1, source_target_pairs={{1,0},{2,1},{3,2},{4,3},{5,4},{6,5},{7,6},{8,7},{9,8},{10,9},{11,1... | collective-permute-start | bytes 155528 | tf_op jit(solution)/shard_map/ppermute | solution.py:17
  104.8 1.6 %copy-start.13 = (pred[48]{0:T(512)(128)(4,1)S(1)}, pred[48]{0:T(512)(128)(4,1)}, u32[]{:S(2)}) copy-start(pred[48]{0:T(512)(128)(4,1)} %iota_compare_fusion.1) | copy-start | bytes 148
  106.0 10.5 %copy-start.2 = (bf16[48,216,216]{2,1,0:T(8,128)(2,1)}, bf16[48,216,216]{2,1,0:T(8,128)(2,1)S(1)}, u32[]{:S(2)}) copy-start(bf16[48,216,216]{2,1,0:T(8,128)(2,1)S(1)} %constant_dynamic-update-slice_fusion.6) | copy-start | bytes 13436932
  116.6 1.0 copy-start.14
  116.6 3.0 %copy-start.5 = (f32[48,5,216]{2,1,0:T(8,128)S(1)}, f32[48,5,216]{2,1,0:T(8,128)}, u32[]{:S(2)}) copy-start(f32[48,5,216]{2,1,0:T(8,128)} %get-tuple-element.33) | copy-start | bytes 622084
  116.6 3.0 %copy-start.8 = (f32[48,6]{1,0:T(8,128)S(1)}, f32[48,6]{1,0:T(8,128)}, u32[]{:S(2)}) copy-start(f32[48,6]{1,0:T(8,128)} %copy.24) | copy-start | bytes 3460
  116.6 3.6 %copy-start.7 = (bf16[48,5,216]{2,1,0:T(8,128)(2,1)S(1)}, bf16[48,5,216]{2,1,0:T(8,128)(2,1)}, u32[]{:S(2)}) copy-start(bf16[48,5,216]{2,1,0:T(8,128)(2,1)} %copy-done.6) | copy-start | bytes 311044
  116.6 3.6 %copy-start.9 = (f32[48,216]{1,0:T(8,128)S(1)}, f32[48,216]{1,0:T(8,128)}, u32[]{:S(2)}) copy-start(f32[48,216]{1,0:T(8,128)} %fusion.29) | copy-start | bytes 124420
  116.6 3.6 %copy-start.15 = (bf16[64,5]{0,1:T(8,128)(2,1)S(1)}, bf16[64,5]{0,1:T(8,128)(2,1)}, u32[]{:S(2)}) copy-start(bf16[64,5]{0,1:T(8,128)(2,1)} %param.16) | copy-start | bytes 1924
  125.1 10.8 %collective-permute-start.16 = (bf16[24,5,216]{2,1,0:T(8,128)(2,1)S(1)}, bf16[24,5,216]{2,1,0:T(8,128)(2,1)S(1)}, u32[]{:S(2)}, u32[]{:S(2)}) collective-permute-start(bf16[24,5,216]{2,1,0:T(8,128)(2,1)S(1)} %get-tuple-element.19), channel_id=1, source_target_pairs={{0,1},{1,2},{2,3},{3,4},{4,5},{5,6},{6,7},{7,8},{8,9},{9,10},{10,1... | collective-permute-start | bytes 155528 | tf_op jit(solution)/shard_map/ppermute | solution.py:16
  127.0 10.1 %collective-permute-start.17 = (bf16[24,5,216]{2,1,0:T(8,128)(2,1)S(1)}, bf16[24,5,216]{2,1,0:T(8,128)(2,1)S(1)}, u32[]{:S(2)}, u32[]{:S(2)}) collective-permute-start(bf16[24,5,216]{2,1,0:T(8,128)(2,1)S(1)} %get-tuple-element.20), channel_id=1, source_target_pairs={{1,0},{2,1},{3,2},{4,3},{5,4},{6,5},{7,6},{8,7},{9,8},{10,9},{11,1... | collective-permute-start | bytes 155528 | tf_op jit(solution)/shard_map/ppermute | solution.py:17
where the time goes:
time: 146 us; the launch traced here: 144 us
  starting transfers between devices  77.3 us (53%)
  local copies, waits for them, and re-layouts  32 us (22%)
  other arithmetic  18.2 us (12%)
  matrix products  12.2 us (8%)
  between operations  3.11 us (2%)
    ppermute x14, starting transfers between devices, from_behind(): return lax.ppermute(shard, axis, pairs)  57.5 us
    ppermute x2, starting transfers between devices, padded_2(): after = lax.ppermute(initial, axis, down)  15.9 us
    select_n x2, other arithmetic, place(): return jnp.where(live, window, jnp.zeros((), values.dtype))  10.3 us
    unnamed x43, local copies, waits for them, and re-layouts  7.63 us
    dot_general x2, matrix products, run_sweeps(): jnp.einsum('enm,evm->evn', tiles_mass, rounded, preferred_element_type=jn...  6.39 us
    dot_general x2, matrix products, run_sweeps(): jnp.einsum('enm,evn->evm', tiles_jac, weighted, preferred_element_type=jn...  4.18 us
    ppermute x2, starting transfers between devices, padded_2(): before = lax.ppermute(last, axis, up)  3.84 us
    gather x2, local copies, waits for them, and re-layouts, run_sweeps(): beside = jnp.take(padded, near_index, axis=0, mode='clip')  3.65 us
  transfers between devices with their start and end apart: 18, of which 1 were waited for; matrix products, arithmetic and copies ran while one was open for 32% of the time, Pallas kernels for 0%

commit v1 on v0

v1 whole, which is shorter than its diff:
```python
import functools

import jax
import jax.numpy as jnp
from jax import lax
from jax.experimental import pallas as pl
from jax.experimental.pallas import tpu as pltpu
from jax.sharding import PartitionSpec as P

SWEEPS = 2
SLOT = 8
MOVE = 8
REACH = 16
LANES = 128
NT = (((1,), (1,)), ((), ()))
NN = (((1,), (0,)), ((), ()))
F32 = jnp.float32
BF16 = jnp.bfloat16


def dot(a, b, dims=NN):
    return lax.dot_general(a, b, dims, preferred_element_type=F32)


def iota(shape, dim):
    return lax.broadcasted_iota(jnp.int32, shape, dim)


def sweep_kernel(
    count,
    state_hbm,
    mass_hbm,
    jac_hbm,
    order_hbm,
    owner_hbm,
    near_hbm,
    penalty_hbm,
    inner_hbm,
    outer_hbm,
    mass,
    jac,
    final,
    info,
    state,
    order,
    owners,
    near,
    penalty,
    inner,
    outer,
    current,
    rounded,
    weighted,
    added,
    keep,
    couple,
    target,
    share,
    first_layer,
    second_layer,
    load_sem,
    tile_sem,
    send_sem,
    recv_sem,
):
    me = lax.axis_index("dom")
    right = lax.rem(me + 1, count)
    left = lax.rem(me + count - 1, count)
    elems, nodes = mass_hbm.shape[0], mass_hbm.shape[2]
    rows = elems * SLOT
    edge = MOVE * SLOT
    halo = REACH * SLOT
    core = pl.ds(MOVE, elems)

    small = [
        pltpu.make_async_copy(src, dst, load_sem.at[i])
        for i, (src, dst) in enumerate(
            [
                (state_hbm, state),
                (order_hbm, order),
                (owner_hbm, owners.at[0]),
                (near_hbm, near),
                (penalty_hbm, penalty),
                (inner_hbm, inner),
                (outer_hbm, outer),
            ]
        )
    ]
    big = [
        pltpu.make_async_copy(mass_hbm, mass.at[core], tile_sem.at[0]),
        pltpu.make_async_copy(jac_hbm, jac.at[core], tile_sem.at[1]),
    ]
    for copy in small + big:
        copy.start()

    barrier = pltpu.get_barrier_semaphore()
    for neighbour in (left, right):
        pl.semaphore_signal(
            barrier, inc=1, device_id=(neighbour,), device_id_type=pl.DeviceIdType.MESH
        )
    pl.semaphore_wait(barrier, 2)

    def send(slot, src, dst, device):
        copy = pltpu.make_async_remote_copy(
            src_ref=src,
            dst_ref=dst,
            send_sem=send_sem.at[slot],
            recv_sem=recv_sem.at[slot],
            device_id=(device,),
            device_id_type=pl.DeviceIdType.MESH,
        )
        copy.start()
        return copy

    tail = pl.ds(elems - MOVE, MOVE)
    head = pl.ds(0, MOVE)
    beyond = pl.ds(MOVE + elems, MOVE)
    bulk = [
        send(0, owner_hbm, owners.at[1], right),
        send(1, owner_hbm, owners.at[2], left),
        send(2, mass_hbm.at[tail], mass.at[head], right),
        send(3, mass_hbm.at[head], mass.at[beyond], left),
        send(4, jac_hbm.at[tail], jac.at[head], right),
        send(5, jac_hbm.at[head], jac.at[beyond], left),
    ]

    for copy in small:
        copy.wait()

    row_of = iota((rows, elems), 0) - SLOT * iota((rows, elems), 1)
    current[...] = sum(
        dot((row_of == var).astype(F32).astype(BF16), state[var]) for var in range(state.shape[0])
    )

    spread = (iota((rows, elems), 0) // SLOT == iota((rows, elems), 1)).astype(F32).astype(BF16)
    base = me * elems - REACH
    local = jnp.where(near[...] < 0, -1, near[...] - base).astype(F32).astype(BF16)
    faces = near.shape[0]
    near_rows = dot(spread, local, NT)
    lane_var = (iota((rows, faces), 0) % SLOT).astype(F32)
    target[...] = near_rows * SLOT + lane_var
    share[...] = dot(spread, penalty[...], NT)
    orders = jnp.broadcast_to(order[...].astype(F32), (SLOT, elems)).astype(BF16)
    limit = dot(spread, orders, NT)[:, 0:1] + 1.0
    limit = limit * limit * limit
    keep[...] = (iota((rows, nodes), 1).astype(F32) < limit).astype(F32)

    span = couple.shape[2]
    step = 32

    def couple_rows(i, _):
        at = pl.ds(pl.multiple_of(i * step, step), step)
        cols = iota((step, span), 1).astype(F32)
        total = jnp.zeros((step, span), F32)
        for face in range(faces):
            hit = cols == target[at, face : face + 1]
            total = total + jnp.where(hit, share[at, face : face + 1], 0.0)
        high = total.astype(BF16)
        couple[0, at, :] = high
        couple[1, at, :] = (total - high.astype(F32)).astype(BF16)
        return 0

    lax.fori_loop(0, rows // step, couple_rows, 0)

    group = 4
    hid = inner.shape[1]
    variables = inner.shape[0]
    wide = group * SLOT
    tall = group * hid
    pick = (iota((variables, wide), 1) % SLOT == iota((variables, wide), 0)).astype(F32).astype(BF16)
    repeat = (iota((hid, tall), 1) % hid == iota((hid, tall), 0)).astype(F32).astype(BF16)
    tn = (((0,), (0,)), ((), ()))
    inner_wide = dot(inner[...], pick, tn).astype(BF16)
    inner_tall = dot(repeat, inner_wide, tn)
    same = iota((tall, wide), 0) // hid == iota((tall, wide), 1) // SLOT
    first_layer[...] = jnp.where(same, inner_tall, 0.0).astype(BF16)
    outer_wide = dot(outer[...], repeat).astype(BF16)
    outer_tall = dot(pick, outer_wide, tn)
    same = iota((wide, tall), 0) // SLOT == iota((wide, tall), 1) // hid
    second_layer[...] = jnp.where(same, outer_tall, 0.0).astype(BF16)

    pairs = elems // 2
    unroll = 4
    upper = iota((2 * SLOT, nodes), 0) < SLOT
    own = halo

    for sweep in range(SWEEPS):
        spot = weighted.at[sweep]
        rounded[...] = current[...].astype(BF16)
        if sweep == 0:
            big[0].wait()

        def weigh(i, _):
            for k in range(unroll):
                pair = i * unroll + k
                at = pl.ds(pl.multiple_of(pair * 2 * SLOT, 2 * SLOT), 2 * SLOT)
                values = rounded[at, :]
                one = dot(values, mass[MOVE + 2 * pair], NT)
                two = dot(values, mass[MOVE + 2 * pair + 1], NT)
                to = pl.ds(pl.multiple_of(own + pair * 2 * SLOT, 2 * SLOT), 2 * SLOT)
                spot[to, :] = jnp.where(upper, one, two).astype(BF16)
            return 0

        lax.fori_loop(0, pairs // unroll // 2, weigh, 0)
        to_left = send(
            6 + 2 * sweep, spot.at[pl.ds(own, halo)], spot.at[pl.ds(own + rows, halo)], left
        )
        lax.fori_loop(pairs // unroll // 2, pairs // unroll, weigh, 0)
        to_right = send(
            7 + 2 * sweep, spot.at[pl.ds(own + rows - halo, halo)], spot.at[pl.ds(0, halo)], right
        )

        def close(i, _):
            at = pl.ds(pl.multiple_of(i * wide, wide), wide)
            hidden = jnp.tanh(dot(first_layer[...], rounded[at, :])).astype(BF16)
            added[at, :] = dot(second_layer[...], hidden)
            return 0

        lax.fori_loop(0, rows // wide, close, 0)
        if sweep == 0:
            big[1].wait()

        def transport(i, _):
            for k in range(unroll):
                pair = i * unroll + k
                at = pl.ds(pl.multiple_of(pair * 2 * SLOT, 2 * SLOT), 2 * SLOT)
                frm = pl.ds(pl.multiple_of(own + pair * 2 * SLOT, 2 * SLOT), 2 * SLOT)
                values = spot[frm, :]
                one = dot(values, jac[MOVE + 2 * pair])
                two = dot(values, jac[MOVE + 2 * pair + 1])
                added[at, :] = added[at, :] + jnp.where(upper, one, two)
            return 0

        lax.fori_loop(0, pairs // unroll, transport, 0)
        to_left.wait()
        to_right.wait()
        block = 64

        def finish(i, _):
            at = pl.ds(pl.multiple_of(i * block, block), block)
            frm = pl.ds(pl.multiple_of(own + i * block, block), block)
            beside = dot(couple[0, at, :], spot[...]) + dot(couple[1, at, :], spot[...])
            total = jnp.sum(share[at, :], axis=1, keepdims=True)
            coupling = beside - total * spot[frm, :].astype(F32)
            value = (current[at, :] + added[at, :] + coupling) * keep[at, :]
            if sweep == SWEEPS - 1:
                to = pl.ds(pl.multiple_of(edge + i * block, block), block)
                final[0, to, :] = value[:, :LANES]
                final[1, to, 0 : nodes - LANES] = value[:, LANES:]
            else:
                current[at, :] = value
            return 0

        lax.fori_loop(0, rows // block, finish, 0)

    last = [
        send(10, final.at[:, pl.ds(rows, edge)], final.at[:, pl.ds(0, edge)], right),
        send(11, final.at[:, pl.ds(edge, edge)], final.at[:, pl.ds(edge + rows, edge)], left),
    ]
    for copy in bulk[:2]:
        copy.wait()

    def tally(hits):
        return jnp.sum(hits.astype(F32), axis=1, keepdims=True)

    from_left = tally(owners[1] == me)
    from_right = tally(owners[2] == me)
    stay = tally(owners[0] == me)
    gone = tally(owners[0] == me - 1)
    filled = stay + from_left + from_right
    leading = gone - from_left + MOVE
    line = iota(info.shape, 0)
    info[...] = jnp.where(line == 0, leading, filled)
    for copy in bulk[2:] + last:
        copy.wait()


def place_kernel(mass, jac, final, info, out_mass, out_jac, out_final, zeros, sem):
    leading = jnp.max(info[0:1, :]).astype(jnp.int32)
    filled = jnp.max(info[1:2, :]).astype(jnp.int32)
    slots = out_mass.shape[0]
    always = slots // 3
    group = zeros.shape[0]
    for src, dst in ((mass, out_mass), (jac, out_jac)):
        pltpu.make_async_copy(
            src.at[pl.ds(leading, always)], dst.at[pl.ds(0, always)], sem
        ).start()
    zeros[...] = jnp.zeros(zeros.shape, zeros.dtype)
    for src, dst in ((mass, out_mass), (jac, out_jac)):
        for start in range(always, slots, group):
            to = dst.at[pl.ds(start, group)]

            @pl.when(filled >= start + group)
            def _():
                pltpu.make_async_copy(src.at[pl.ds(leading + start, group)], to, sem).start()

            @pl.when(filled <= start)
            def _():
                pltpu.make_async_copy(zeros, to, sem).start()

            @pl.when((filled > start) & (filled < start + group))
            def _():
                def live(i, _):
                    pltpu.make_async_copy(src.at[leading + i], dst.at[i], sem).start()
                    return 0

                def dead(i, _):
                    pltpu.make_async_copy(zeros.at[0], dst.at[i], sem).start()
                    return 0

                lax.fori_loop(start, filled, live, 0)
                lax.fori_loop(filled, start + group, dead, 0)

    variables = out_final.shape[0]
    nodes = out_final.shape[2]
    alive = iota((slots, LANES), 0) < filled
    for var in range(variables):
        at = pl.ds(leading * SLOT + var, slots, stride=SLOT)
        out_final[var, :, 0:LANES] = jnp.where(alive, final[0, at, :], 0.0)
        out_final[var, :, LANES:nodes] = jnp.where(alive, final[1, at, :], 0.0)[:, : nodes - LANES]
    for dst in (out_mass, out_jac):
        pltpu.make_async_copy(dst, dst, sem).wait()


def shards(
    elem_state,
    mass_inverse,
    jacobian,
    elem_order,
    new_owner,
    neighbors,
    penalty,
    closure_in,
    closure_out,
):
    elems, variables, nodes = elem_state.shape
    hid = closure_in.shape[0]
    faces = neighbors.shape[1]
    count = lax.axis_size("dom")
    slots = elems + 2 * MOVE
    rows = elems * SLOT
    span = rows + 2 * REACH * SLOT
    anywhere = pl.BlockSpec(memory_space=pl.ANY)
    near_by = pl.BlockSpec(memory_space=pltpu.VMEM)
    dma = pltpu.SemaphoreType.DMA
    mass, jac, final, info = pl.pallas_call(
        functools.partial(sweep_kernel, count),
        out_shape=(
            pltpu.VMEM((slots, nodes, nodes), BF16),
            pltpu.VMEM((slots, nodes, nodes), BF16),
            pltpu.VMEM((2, (slots + 2 * MOVE) * SLOT, LANES), F32),
            pltpu.VMEM((8, 128), F32),
        ),
        in_specs=[anywhere] * 9,
        out_specs=(near_by,) * 4,
        scratch_shapes=[
            pltpu.VMEM((variables, elems, nodes), BF16),
            pltpu.VMEM((1, elems), jnp.int32),
            pltpu.VMEM((3, 1, elems), jnp.int32),
            pltpu.VMEM((faces, elems), jnp.int32),
            pltpu.VMEM((faces, elems), BF16),
            pltpu.VMEM((variables, hid), BF16),
            pltpu.VMEM((variables, hid), BF16),
            pltpu.VMEM((rows, nodes), F32),
            pltpu.VMEM((rows, nodes), BF16),
            pltpu.VMEM((SWEEPS, span, nodes), BF16),
            pltpu.VMEM((rows, nodes), F32),
            pltpu.VMEM((rows, nodes), F32),
            pltpu.VMEM((2, rows, span), BF16),
            pltpu.VMEM((rows, faces), F32),
            pltpu.VMEM((rows, faces), F32),
            pltpu.VMEM((4 * hid, 4 * SLOT), BF16),
            pltpu.VMEM((4 * SLOT, 4 * hid), BF16),
            dma((7,)),
            dma((2,)),
            dma((12,)),
            dma((12,)),
        ],
        compiler_params=pltpu.CompilerParams(
            collective_id=0, has_side_effects=True, vmem_limit_bytes=24 * 2**20
        ),
        name="sweeps",
    )(
        jnp.transpose(elem_state, (1, 0, 2)),
        mass_inverse,
        jacobian,
        elem_order.reshape(1, elems),
        new_owner.reshape(1, elems),
        neighbors.T,
        penalty.T,
        closure_in.T,
        closure_out,
    )
    out_mass, out_jac, out_final = pl.pallas_call(
        place_kernel,
        out_shape=(
            jax.ShapeDtypeStruct((slots, nodes, nodes), BF16),
            jax.ShapeDtypeStruct((slots, nodes, nodes), BF16),
            jax.ShapeDtypeStruct((variables, slots, nodes), F32),
        ),
        in_specs=[near_by] * 4,
        out_specs=(anywhere, anywhere, near_by),
        scratch_shapes=[pltpu.VMEM((8, nodes, nodes), BF16), dma],
        compiler_params=pltpu.CompilerParams(vmem_limit_bytes=24 * 2**20),
        name="place",
    )(mass, jac, final, info)
    return (jnp.transpose(out_final, (1, 0, 2)), out_mass, out_jac)


def solution(mesh):
    placed = (
        P("dom", None, None),
        P("dom", None, None),
        P("dom", None, None),
        P("dom"),
        P("dom"),
        P("dom", None),
        P("dom", None),
        P(),
        P(),
    )
    return jax.shard_map(
        shards,
        mesh=mesh,
        in_specs=placed,
        out_specs=(P("dom", None, None), P("dom", None, None), P("dom", None, None)),
        check_vma=False,
    )
```

time: 146 us -> 60.7 us (0.42)
  the two profiles are of different devices: /device:TPU:24 before, /device:TPU:0 now
where the time goes in v1:
time: 60.7 us; the launch traced here: 60.4 us
  Pallas kernels  50.8 us (84%)
  local copies, waits for them, and re-layouts  8.92 us (15%)
  between operations  0.66 us (1%)
    pallas_call x1, Pallas kernels, shards(): pl.pallas_call(functools.partial(sweep_kernel, count), out_shape=(pltpu.V...  46 us
    unnamed x18, local copies, waits for them, and re-layouts  8.92 us
    pallas_call x1, Pallas kernels, shards(): pl.pallas_call(place_kernel, out_shape=(jax.ShapeDtypeStruct((slots, node...  4.78 us

profile of v1, /device:TPU:0, one launch (start us, length us, event | category | flops | bytes accessed | tf_op | source)
XLA Modules:
  0.0 60.4 jit_solution(17871475781283011946)
XLA Ops:
  0.6 0.0 copy-start
  0.6 2.0 %copy-done = bf16[32,216,216]{2,1,0:T(8,128)(2,1)S(1)} copy-done((bf16[32,216,216]{2,1,0:T(8,128)(2,1)S(1)}, bf16[32,216,216]{2,1,0:T(8,128)(2,1)}, u32[]{:S(2)}) %copy-start) | copy-done | bytes 2986008
  2.6 0.0 copy-start.1
  2.6 2.0 %copy-done.1 = bf16[32,216,216]{2,1,0:T(8,128)(2,1)S(1)} copy-done((bf16[32,216,216]{2,1,0:T(8,128)(2,1)S(1)}, bf16[32,216,216]{2,1,0:T(8,128)(2,1)}, u32[]{:S(2)}) %copy-start.1) | copy-done | bytes 2986008
  4.6 0.0 copy-start.2
  4.6 0.9 %copy-done.2 = bf16[32,5,216]{2,0,1:T(8,128)(2,1)S(1)} copy-done((bf16[32,5,216]{2,0,1:T(8,128)(2,1)S(1)}, bf16[32,5,216]{2,0,1:T(8,128)(2,1)}, u32[]{:S(2)}) %copy-start.2) | copy-done | bytes 69144
  5.5 0.0 copy-start.3
  5.5 0.7 %copy-done.3 = s32[32,6]{0,1:T(8,128)S(1)} copy-done((s32[32,6]{0,1:T(8,128)S(1)}, s32[32,6]{0,1:T(8,128)}, u32[]{:S(2)}) %copy-start.3) | copy-done | bytes 792
  6.2 0.0 copy-start.4
  6.2 0.7 %copy-done.4 = bf16[32,6]{0,1:T(8,128)(2,1)S(1)} copy-done((bf16[32,6]{0,1:T(8,128)(2,1)S(1)}, bf16[32,6]{0,1:T(8,128)(2,1)}, u32[]{:S(2)}) %copy-start.4) | copy-done | bytes 408
  6.9 0.0 copy-start.5
  6.9 0.7 %copy-done.5 = bf16[64,5]{0,1:T(8,128)(2,1)S(1)} copy-done((bf16[64,5]{0,1:T(8,128)(2,1)S(1)}, bf16[64,5]{0,1:T(8,128)(2,1)}, u32[]{:S(2)}) %copy-start.5) | copy-done | bytes 664
  7.6 0.0 copy-start.6
  7.6 0.7 %copy-done.6 = bf16[5,64]{1,0:T(8,128)(2,1)S(1)} copy-done((bf16[5,64]{1,0:T(8,128)(2,1)S(1)}, bf16[5,64]{1,0:T(8,128)(2,1)}, u32[]{:S(2)}) %copy-start.6) | copy-done | bytes 664
  8.3 0.0 copy-start.7
  8.3 0.7 %copy-done.7 = s32[32]{0:T(128)S(1)} copy-done((s32[32]{0:T(128)S(1)}, s32[32]{0:T(128)}, u32[]{:S(2)}) %copy-start.7) | copy-done | bytes 152
  8.9 0.0 copy-start.8
  8.9 0.7 %copy-done.8 = s32[32]{0:T(128)S(1)} copy-done((s32[32]{0:T(128)S(1)}, s32[32]{0:T(128)}, u32[]{:S(2)}) %copy-start.8) | copy-done | bytes 152
  9.6 46.0 %sweeps.1 = (bf16[48,216,216]{2,1,0:T(8,128)(2,1)S(1)}, bf16[48,216,216]{2,1,0:T(8,128)(2,1)S(1)}, f32[2,512,128]{2,1,0:T(8,128)S(1)}, f32[8,128]{1,0:T(8,128)S(1)}) custom-call(bf16[5,32,216]{2,1,0:T(8,128)(2,1)S(1)} %bitcast.7, bf16[32,216,216]{2,1,0:T(8,128)(2,1)S(1)} %copy-done, bf16[32,216,216]{2,1,0:T(8,128)(2,1)S(1)} %copy-done.1, ...), custom_call_target="tpu_custom_call" | custom-call | tf_op jit(solution)/shard_map/sweeps/pallas_call | solution.py:346
  55.6 4.8 %place.1 = (bf16[48,216,216]{2,1,0:T(8,128)(2,1)}, bf16[48,216,216]{2,1,0:T(8,128)(2,1)}, f32[5,48,216]{2,1,0:T(8,128)}) custom-call(bf16[48,216,216]{2,1,0:T(8,128)(2,1)S(1)} %get-tuple-element.10.mass, bf16[48,216,216]{2,1,0:T(8,128)(2,1)S(1)} %get-tuple-element.11.jac, f32[2,512,128]{2,1,0:T(8,128)S(1)} %get-tuple-element.12.final, ...), custom_call_target="tpu_custom_call" | custom-call | tf_op jit(solution)/shard_map/place/pallas_call | solution.py:394
Async XLA Ops:
  0.6 2.0 %copy-start = (bf16[32,216,216]{2,1,0:T(8,128)(2,1)S(1)}, bf16[32,216,216]{2,1,0:T(8,128)(2,1)}, u32[]{:S(2)}) copy-start(bf16[32,216,216]{2,1,0:T(8,128)(2,1)} %mass_hbm.1) | copy-start | bytes 8957956
  2.6 2.0 %copy-start.1 = (bf16[32,216,216]{2,1,0:T(8,128)(2,1)S(1)}, bf16[32,216,216]{2,1,0:T(8,128)(2,1)}, u32[]{:S(2)}) copy-start(bf16[32,216,216]{2,1,0:T(8,128)(2,1)} %jac_hbm.1) | copy-start | bytes 8957956
  4.6 0.9 %copy-start.2 = (bf16[32,5,216]{2,0,1:T(8,128)(2,1)S(1)}, bf16[32,5,216]{2,0,1:T(8,128)(2,1)}, u32[]{:S(2)}) copy-start(bf16[32,5,216]{2,0,1:T(8,128)(2,1)} %param.9) | copy-start | bytes 207364
  5.5 0.7 %copy-start.3 = (s32[32,6]{0,1:T(8,128)S(1)}, s32[32,6]{0,1:T(8,128)}, u32[]{:S(2)}) copy-start(s32[32,6]{0,1:T(8,128)} %param.14) | copy-start | bytes 2308
  6.2 0.7 %copy-start.4 = (bf16[32,6]{0,1:T(8,128)(2,1)S(1)}, bf16[32,6]{0,1:T(8,128)(2,1)}, u32[]{:S(2)}) copy-start(bf16[32,6]{0,1:T(8,128)(2,1)} %param.15) | copy-start | bytes 1156
  6.9 0.7 %copy-start.5 = (bf16[64,5]{0,1:T(8,128)(2,1)S(1)}, bf16[64,5]{0,1:T(8,128)(2,1)}, u32[]{:S(2)}) copy-start(bf16[64,5]{0,1:T(8,128)(2,1)} %param.16) | copy-start | bytes 1924
  7.6 0.7 %copy-start.6 = (bf16[5,64]{1,0:T(8,128)(2,1)S(1)}, bf16[5,64]{1,0:T(8,128)(2,1)}, u32[]{:S(2)}) copy-start(bf16[5,64]{1,0:T(8,128)(2,1)} %outer_hbm.1) | copy-start | bytes 1924
  8.3 0.7 %copy-start.7 = (s32[32]{0:T(128)S(1)}, s32[32]{0:T(128)}, u32[]{:S(2)}) copy-start(s32[32]{0:T(128)} %param.12) | copy-start | bytes 388
  8.9 0.7 %copy-start.8 = (s32[32]{0:T(128)S(1)}, s32[32]{0:T(128)}, u32[]{:S(2)}) copy-start(s32[32]{0:T(128)} %param.13) | copy-start | bytes 388

commit v2 on v1

--- a/solution.py
+++ b/solution.py
@@ -93,15 +93,27 @@
     for copy in small + big:
         copy.start()
 
+    has_left = me > 0
+    has_right = me < count - 1
     barrier = pltpu.get_barrier_semaphore()
-    for neighbour in (left, right):
+
+    def greet(device):
         pl.semaphore_signal(
-            barrier, inc=1, device_id=(neighbour,), device_id_type=pl.DeviceIdType.MESH
+            barrier, inc=1, device_id=(device,), device_id_type=pl.DeviceIdType.MESH
         )
-    pl.semaphore_wait(barrier, 2)
-
-    def send(slot, src, dst, device):
-        copy = pltpu.make_async_remote_copy(
+
+    @pl.when(has_left)
+    def _():
+        greet(me - 1)
+
+    @pl.when(has_right)
+    def _():
+        greet(me + 1)
+
+    pl.semaphore_wait(barrier, has_left.astype(jnp.int32) + has_right.astype(jnp.int32))
+
+    def sender(slot, src, dst, device):
+        return pltpu.make_async_remote_copy(
             src_ref=src,
             dst_ref=dst,
             send_sem=send_sem.at[slot],
@@ -109,20 +121,48 @@
             device_id=(device,),
             device_id_type=pl.DeviceIdType.MESH,
         )
-        copy.start()
-        return copy
+
+    class ToRight:
+        def __init__(self, slot, src, dst):
+            self.copy = sender(slot, src, dst, right)
+            pl.when(has_right)(self.copy.start)
+
+        def wait(self):
+            pl.when(has_right)(self.copy.wait_send)
+            pl.when(has_left)(self.copy.wait_recv)
+
+    class ToLeft:
+        def __init__(self, slot, src, dst):
+            self.copy = sender(slot, src, dst, left)
+            pl.when(has_left)(self.copy.start)
+
+        def wait(self):
+            pl.when(has_left)(self.copy.wait_send)
+            pl.when(has_right)(self.copy.wait_recv)
 
     tail = pl.ds(elems - MOVE, MOVE)
     head = pl.ds(0, MOVE)
     beyond = pl.ds(MOVE + elems, MOVE)
     bulk = [
-        send(0, owner_hbm, owners.at[1], right),
-        send(1, owner_hbm, owners.at[2], left),
-        send(2, mass_hbm.at[tail], mass.at[head], right),
-        send(3, mass_hbm.at[head], mass.at[beyond], left),
-        send(4, jac_hbm.at[tail], jac.at[head], right),
-        send(5, jac_hbm.at[head], jac.at[beyond], left),
+        ToRight(0, owner_hbm, owners.at[1]),
+        ToLeft(1, owner_hbm, owners.at[2]),
+        ToRight(2, mass_hbm.at[tail], mass.at[head]),
+        ToLeft(3, mass_hbm.at[head], mass.at[beyond]),
+        ToRight(4, jac_hbm.at[tail], jac.at[head]),
+        ToLeft(5, jac_hbm.at[head], jac.at[beyond]),
     ]
+
+    @pl.when(jnp.logical_not(has_left))
+    def _():
+        for sweep in range(SWEEPS):
+            weighted[sweep, 0:halo, :] = jnp.zeros((halo, nodes), BF16)
+        owners[1] = jnp.full((1, elems), -1, jnp.int32)
+
+    @pl.when(jnp.logical_not(has_right))
+    def _():
+        for sweep in range(SWEEPS):
+            weighted[sweep, halo + rows : 2 * halo + rows, :] = jnp.zeros((halo, nodes), BF16)
+        owners[2] = jnp.full((1, elems), -1, jnp.int32)
 
     for copy in small:
         copy.wait()
@@ -202,12 +242,12 @@
             return 0
 
         lax.fori_loop(0, pairs // unroll // 2, weigh, 0)
-        to_left = send(
-            6 + 2 * sweep, spot.at[pl.ds(own, halo)], spot.at[pl.ds(own + rows, halo)], left
+        to_left = ToLeft(
+            6 + 2 * sweep, spot.at[pl.ds(own, halo)], spot.at[pl.ds(own + rows, halo)]
         )
         lax.fori_loop(pairs // unroll // 2, pairs // unroll, weigh, 0)
-        to_right = send(
-            7 + 2 * sweep, spot.at[pl.ds(own + rows - halo, halo)], spot.at[pl.ds(0, halo)], right
+        to_right = ToRight(
+            7 + 2 * sweep, spot.at[pl.ds(own + rows - halo, halo)], spot.at[pl.ds(0, halo)]
         )
 
         def close(i, _):
@@ -254,8 +294,8 @@
         lax.fori_loop(0, rows // block, finish, 0)
 
     last = [
-        send(10, final.at[:, pl.ds(rows, edge)], final.at[:, pl.ds(0, edge)], right),
-        send(11, final.at[:, pl.ds(edge, edge)], final.at[:, pl.ds(edge + rows, edge)], left),
+        ToRight(10, final.at[:, pl.ds(rows, edge)], final.at[:, pl.ds(0, edge)]),
+        ToLeft(11, final.at[:, pl.ds(edge, edge)], final.at[:, pl.ds(edge + rows, edge)]),
     ]
     for copy in bulk[:2]:
         copy.wait()
@@ -340,7 +380,18 @@
     slots = elems + 2 * MOVE
     rows = elems * SLOT
     span = rows + 2 * REACH * SLOT
-    anywhere = pl.BlockSpec(memory_space=pl.ANY)
+    operands = (
+        jnp.transpose(elem_state, (1, 0, 2)),
+        mass_inverse,
+        jacobian,
+        elem_order.reshape(1, elems),
+        new_owner.reshape(1, elems),
+        neighbors.T,
+        penalty.T,
+        closure_in.T,
+        closure_out,
+    )
+    anywhere = pl.BlockSpec(memory_space=pltpu.HBM)
     near_by = pl.BlockSpec(memory_space=pltpu.VMEM)
     dma = pltpu.SemaphoreType.DMA
     mass, jac, final, info = pl.pallas_call(
@@ -380,17 +431,7 @@
             collective_id=0, has_side_effects=True, vmem_limit_bytes=24 * 2**20
         ),
         name="sweeps",
-    )(
-        jnp.transpose(elem_state, (1, 0, 2)),
-        mass_inverse,
-        jacobian,
-        elem_order.reshape(1, elems),
-        new_owner.reshape(1, elems),
-        neighbors.T,
-        penalty.T,
-        closure_in.T,
-        closure_out,
-    )
+    )(*(pltpu.with_memory_space_constraint(operand, pltpu.HBM) for operand in operands))
     out_mass, out_jac, out_final = pl.pallas_call(
         place_kernel,
         out_shape=(

time: 60.7 us -> 47.4 us (0.78)
  the two profiles are of different devices: /device:TPU:0 before, /device:TPU:24 now
where the time goes in v2:
time: 47.4 us; the launch traced here: 47.3 us
  Pallas kernels  46.7 us (99%)
  between operations  0.64 us (1%)
    pallas_call x1, Pallas kernels, shards(): pl.pallas_call(functools.partial(sweep_kernel, count), out_shape=(pltpu.V...  41.9 us
    pallas_call x1, Pallas kernels, shards(): pl.pallas_call(place_kernel, out_shape=(jax.ShapeDtypeStruct((slots, node...  4.78 us

profile of v2, /device:TPU:24, one launch (start us, length us, event | category | flops | bytes accessed | tf_op | source)
XLA Modules:
  0.0 47.3 jit_solution(12482744597538797442)
XLA Ops:
  0.6 41.9 %sweeps.1 = (bf16[48,216,216]{2,1,0:T(8,128)(2,1)S(1)}, bf16[48,216,216]{2,1,0:T(8,128)(2,1)S(1)}, f32[2,512,128]{2,1,0:T(8,128)S(1)}, f32[8,128]{1,0:T(8,128)S(1)}) custom-call(bf16[5,32,216]{2,1,0:T(8,128)(2,1)} %bitcast.7, bf16[32,216,216]{2,1,0:T(8,128)(2,1)} %mass_hbm.1, bf16[32,216,216]{2,1,0:T(8,128)(2,1)} %jac_hbm.1, s32[1,32]{1,0:T(1,128)} %bitcast.11, ...), custom_call_target="tpu_custom_call" | custom-call | tf_op jit(solution)/shard_map/sweeps/pallas_call | solution.py:397
  42.5 4.8 %place.1 = (bf16[48,216,216]{2,1,0:T(8,128)(2,1)}, bf16[48,216,216]{2,1,0:T(8,128)(2,1)}, f32[5,48,216]{2,1,0:T(8,128)}) custom-call(bf16[48,216,216]{2,1,0:T(8,128)(2,1)S(1)} %get-tuple-element.10.mass, bf16[48,216,216]{2,1,0:T(8,128)(2,1)S(1)} %get-tuple-element.11.jac, f32[2,512,128]{2,1,0:T(8,128)S(1)} %get-tuple-element.12.final, ...), custom_call_target="tpu_custom_call" | custom-call | tf_op jit(solution)/shard_map/place/pallas_call | solution.py:435

commit v3 on v2

--- a/solution.py
+++ b/solution.py
@@ -12,6 +12,14 @@
 MOVE = 8
 REACH = 16
 LANES = 128
+SCHEDULE = (
+    ((0, 0, 3),),
+    ((0, 3, 5), (1, 0, 1)),
+    ((1, 1, 4),),
+    ((1, 5, 3),),
+)
+SENDS = 8 + 2 * sum(len(part) for part in SCHEDULE)
+CLOSE = 2
 NT = (((1,), (1,)), ((), ()))
 NN = (((1,), (0,)), ((), ()))
 F32 = jnp.float32
@@ -86,11 +94,17 @@
             ]
         )
     ]
-    big = [
-        pltpu.make_async_copy(mass_hbm, mass.at[core], tile_sem.at[0]),
-        pltpu.make_async_copy(jac_hbm, jac.at[core], tile_sem.at[1]),
+    half = elems // 2
+    mass_load = [
+        pltpu.make_async_copy(
+            mass_hbm.at[pl.ds(i * half, half)],
+            mass.at[pl.ds(MOVE + i * half, half)],
+            tile_sem.at[i],
+        )
+        for i in range(2)
     ]
-    for copy in small + big:
+    jac_load = pltpu.make_async_copy(jac_hbm, jac.at[core], tile_sem.at[2])
+    for copy in small + mass_load + [jac_load]:
         copy.start()
 
     has_left = me > 0
@@ -140,17 +154,29 @@
             pl.when(has_left)(self.copy.wait_send)
             pl.when(has_right)(self.copy.wait_recv)
 
-    tail = pl.ds(elems - MOVE, MOVE)
-    head = pl.ds(0, MOVE)
-    beyond = pl.ds(MOVE + elems, MOVE)
-    bulk = [
-        ToRight(0, owner_hbm, owners.at[1]),
-        ToLeft(1, owner_hbm, owners.at[2]),
-        ToRight(2, mass_hbm.at[tail], mass.at[head]),
-        ToLeft(3, mass_hbm.at[head], mass.at[beyond]),
-        ToRight(4, jac_hbm.at[tail], jac.at[head]),
-        ToLeft(5, jac_hbm.at[head], jac.at[beyond]),
-    ]
+    meta = [ToRight(0, owner_hbm, owners.at[1]), ToLeft(1, owner_hbm, owners.at[2])]
+    bulk = []
+
+    def tiles(phase):
+        for which, start, size in SCHEDULE[phase]:
+            src, dst = ((mass_hbm, mass), (jac_hbm, jac))[which]
+            slot = 8 + len(bulk)
+            bulk.append(
+                ToRight(
+                    slot,
+                    src.at[pl.ds(elems - MOVE + start, size)],
+                    dst.at[pl.ds(start, size)],
+                )
+            )
+            bulk.append(
+                ToLeft(
+                    slot + 1,
+                    src.at[pl.ds(start, size)],
+                    dst.at[pl.ds(MOVE + elems + start, size)],
+                )
+            )
+
+    tiles(0)
 
     @pl.when(jnp.logical_not(has_left))
     def _():
@@ -164,60 +190,63 @@
             weighted[sweep, halo + rows : 2 * halo + rows, :] = jnp.zeros((halo, nodes), BF16)
         owners[2] = jnp.full((1, elems), -1, jnp.int32)
 
-    for copy in small:
-        copy.wait()
+    small[0].wait()
 
     row_of = iota((rows, elems), 0) - SLOT * iota((rows, elems), 1)
     current[...] = sum(
         dot((row_of == var).astype(F32).astype(BF16), state[var]) for var in range(state.shape[0])
     )
-
-    spread = (iota((rows, elems), 0) // SLOT == iota((rows, elems), 1)).astype(F32).astype(BF16)
-    base = me * elems - REACH
-    local = jnp.where(near[...] < 0, -1, near[...] - base).astype(F32).astype(BF16)
-    faces = near.shape[0]
-    near_rows = dot(spread, local, NT)
-    lane_var = (iota((rows, faces), 0) % SLOT).astype(F32)
-    target[...] = near_rows * SLOT + lane_var
-    share[...] = dot(spread, penalty[...], NT)
-    orders = jnp.broadcast_to(order[...].astype(F32), (SLOT, elems)).astype(BF16)
-    limit = dot(spread, orders, NT)[:, 0:1] + 1.0
-    limit = limit * limit * limit
-    keep[...] = (iota((rows, nodes), 1).astype(F32) < limit).astype(F32)
-
-    span = couple.shape[2]
-    step = 32
-
-    def couple_rows(i, _):
-        at = pl.ds(pl.multiple_of(i * step, step), step)
-        cols = iota((step, span), 1).astype(F32)
-        total = jnp.zeros((step, span), F32)
-        for face in range(faces):
-            hit = cols == target[at, face : face + 1]
-            total = total + jnp.where(hit, share[at, face : face + 1], 0.0)
-        high = total.astype(BF16)
-        couple[0, at, :] = high
-        couple[1, at, :] = (total - high.astype(F32)).astype(BF16)
-        return 0
-
-    lax.fori_loop(0, rows // step, couple_rows, 0)
 
     group = 4
     hid = inner.shape[1]
     variables = inner.shape[0]
     wide = group * SLOT
     tall = group * hid
-    pick = (iota((variables, wide), 1) % SLOT == iota((variables, wide), 0)).astype(F32).astype(BF16)
-    repeat = (iota((hid, tall), 1) % hid == iota((hid, tall), 0)).astype(F32).astype(BF16)
-    tn = (((0,), (0,)), ((), ()))
-    inner_wide = dot(inner[...], pick, tn).astype(BF16)
-    inner_tall = dot(repeat, inner_wide, tn)
-    same = iota((tall, wide), 0) // hid == iota((tall, wide), 1) // SLOT
-    first_layer[...] = jnp.where(same, inner_tall, 0.0).astype(BF16)
-    outer_wide = dot(outer[...], repeat).astype(BF16)
-    outer_tall = dot(pick, outer_wide, tn)
-    same = iota((wide, tall), 0) // SLOT == iota((wide, tall), 1) // hid
-    second_layer[...] = jnp.where(same, outer_tall, 0.0).astype(BF16)
+    def prepare():
+        for copy in small[1:]:
+            copy.wait()
+
+        spread = (iota((rows, elems), 0) // SLOT == iota((rows, elems), 1)).astype(F32).astype(BF16)
+        base = me * elems - REACH
+        local = jnp.where(near[...] < 0, -1, near[...] - base).astype(F32).astype(BF16)
+        faces = near.shape[0]
+        near_rows = dot(spread, local, NT)
+        lane_var = (iota((rows, faces), 0) % SLOT).astype(F32)
+        target[...] = near_rows * SLOT + lane_var
+        share[...] = dot(spread, penalty[...], NT)
+        orders = jnp.broadcast_to(order[...].astype(F32), (SLOT, elems)).astype(BF16)
+        limit = dot(spread, orders, NT)[:, 0:1] + 1.0
+        limit = limit * limit * limit
+        keep[...] = (iota((rows, nodes), 1).astype(F32) < limit).astype(F32)
+
+        span = couple.shape[2]
+        step = 32
+
+        def couple_rows(i, _):
+            at = pl.ds(pl.multiple_of(i * step, step), step)
+            cols = iota((step, span), 1).astype(F32)
+            total = jnp.zeros((step, span), F32)
+            for face in range(faces):
+                hit = cols == target[at, face : face + 1]
+                total = total + jnp.where(hit, share[at, face : face + 1], 0.0)
+            high = total.astype(BF16)
+            couple[0, at, :] = high
+            couple[1, at, :] = (total - high.astype(F32)).astype(BF16)
+            return 0
+
+        lax.fori_loop(0, rows // step, couple_rows, 0)
+
+        pick = (iota((variables, wide), 1) % SLOT == iota((variables, wide), 0)).astype(F32).astype(BF16)
+        repeat = (iota((hid, tall), 1) % hid == iota((hid, tall), 0)).astype(F32).astype(BF16)
+        tn = (((0,), (0,)), ((), ()))
+        inner_wide = dot(inner[...], pick, tn).astype(BF16)
+        inner_tall = dot(repeat, inner_wide, tn)
+        same = iota((tall, wide), 0) // hid == iota((tall, wide), 1) // SLOT
+        first_layer[...] = jnp.where(same, inner_tall, 0.0).astype(BF16)
+        outer_wide = dot(outer[...], repeat).astype(BF16)
+        outer_tall = dot(pick, outer_wide, tn)
+        same = iota((wide, tall), 0) // SLOT == iota((wide, tall), 1) // hid
+        second_layer[...] = jnp.where(same, outer_tall, 0.0).astype(BF16)
 
     pairs = elems // 2
     unroll = 4
@@ -228,7 +257,7 @@
         spot = weighted.at[sweep]
         rounded[...] = current[...].astype(BF16)
         if sweep == 0:
-            big[0].wait()
+            mass_load[0].wait()
 
         def weigh(i, _):
             for k in range(unroll):
@@ -243,22 +272,32 @@
 
         lax.fori_loop(0, pairs // unroll // 2, weigh, 0)
         to_left = ToLeft(
-            6 + 2 * sweep, spot.at[pl.ds(own, halo)], spot.at[pl.ds(own + rows, halo)]
+            2 + 2 * sweep, spot.at[pl.ds(own, halo)], spot.at[pl.ds(own + rows, halo)]
         )
+        if sweep == 0:
+            mass_load[1].wait()
         lax.fori_loop(pairs // unroll // 2, pairs // unroll, weigh, 0)
         to_right = ToRight(
-            7 + 2 * sweep, spot.at[pl.ds(own + rows - halo, halo)], spot.at[pl.ds(0, halo)]
+            3 + 2 * sweep, spot.at[pl.ds(own + rows - halo, halo)], spot.at[pl.ds(0, halo)]
         )
 
+        tiles(sweep + 1)
+        if sweep == 0:
+            prepare()
+
         def close(i, _):
-            at = pl.ds(pl.multiple_of(i * wide, wide), wide)
-            hidden = jnp.tanh(dot(first_layer[...], rounded[at, :])).astype(BF16)
-            added[at, :] = dot(second_layer[...], hidden)
+            ats = [
+                pl.ds(pl.multiple_of((i * CLOSE + k) * wide, wide), wide) for k in range(CLOSE)
+            ]
+            inputs = [dot(first_layer[...], rounded[at, :]) for at in ats]
+            hidden = [jnp.tanh(value).astype(BF16) for value in inputs]
+            for at, value in zip(ats, hidden):
+                added[at, :] = dot(second_layer[...], value)
             return 0
 
-        lax.fori_loop(0, rows // wide, close, 0)
+        lax.fori_loop(0, rows // wide // CLOSE, close, 0)
         if sweep == 0:
-            big[1].wait()
+            jac_load.wait()
 
         def transport(i, _):
             for k in range(unroll):
@@ -294,10 +333,11 @@
         lax.fori_loop(0, rows // block, finish, 0)
 
     last = [
-        ToRight(10, final.at[:, pl.ds(rows, edge)], final.at[:, pl.ds(0, edge)]),
-        ToLeft(11, final.at[:, pl.ds(edge, edge)], final.at[:, pl.ds(edge + rows, edge)]),
+        ToRight(6, final.at[:, pl.ds(rows, edge)], final.at[:, pl.ds(0, edge)]),
+        ToLeft(7, final.at[:, pl.ds(edge, edge)], final.at[:, pl.ds(edge + rows, edge)]),
     ]
-    for copy in bulk[:2]:
+    tiles(SWEEPS + 1)
+    for copy in meta:
         copy.wait()
 
     def tally(hits):
@@ -311,7 +351,7 @@
     leading = gone - from_left + MOVE
     line = iota(info.shape, 0)
     info[...] = jnp.where(line == 0, leading, filled)
-    for copy in bulk[2:] + last:
+    for copy in last + bulk:
         copy.wait()
 
 
@@ -423,9 +463,9 @@
             pltpu.VMEM((4 * hid, 4 * SLOT), BF16),
             pltpu.VMEM((4 * SLOT, 4 * hid), BF16),
             dma((7,)),
-            dma((2,)),
-            dma((12,)),
-            dma((12,)),
+            dma((3,)),
+            dma((SENDS,)),
+            dma((SENDS,)),
         ],
         compiler_params=pltpu.CompilerParams(
             collective_id=0, has_side_effects=True, vmem_limit_bytes=24 * 2**20

time: 47.4 us -> 37.7 us (0.80)
  Pallas kernels: 46.7 us -> 37 us
    pallas_call x1, Pallas kernels: 41.9 us -> 32.2 us  [shards(): pl.pallas_call(functools.partial(sweep_kernel, count), out_shape=(pltpu.V...]
where the time goes in v3:
time: 37.7 us; the launch traced here: 37.6 us
  Pallas kernels  37 us (98%)
  between operations  0.64 us (2%)
    pallas_call x1, Pallas kernels, shards(): pl.pallas_call(functools.partial(sweep_kernel, count), out_shape=(pltpu.V...  32.2 us
    pallas_call x1, Pallas kernels, shards(): pl.pallas_call(place_kernel, out_shape=(jax.ShapeDtypeStruct((slots, node...  4.78 us

profile of v3, /device:TPU:24, one launch (start us, length us, event | category | flops | bytes accessed | tf_op | source)
XLA Modules:
  0.0 37.6 jit_solution(8912575557814848867)
XLA Ops:
  0.6 32.2 %sweeps.1 = (bf16[48,216,216]{2,1,0:T(8,128)(2,1)S(1)}, bf16[48,216,216]{2,1,0:T(8,128)(2,1)S(1)}, f32[2,512,128]{2,1,0:T(8,128)S(1)}, f32[8,128]{1,0:T(8,128)S(1)}) custom-call(bf16[5,32,216]{2,1,0:T(8,128)(2,1)} %bitcast.7, bf16[32,216,216]{2,1,0:T(8,128)(2,1)} %mass_hbm.1, bf16[32,216,216]{2,1,0:T(8,128)(2,1)} %jac_hbm.1, s32[1,32]{1,0:T(1,128)} %bitcast.11, ...), custom_call_target="tpu_custom_call" | custom-call | tf_op jit(solution)/shard_map/sweeps/pallas_call | solution.py:437
  32.8 4.8 %place.1 = (bf16[48,216,216]{2,1,0:T(8,128)(2,1)}, bf16[48,216,216]{2,1,0:T(8,128)(2,1)}, f32[5,48,216]{2,1,0:T(8,128)}) custom-call(bf16[48,216,216]{2,1,0:T(8,128)(2,1)S(1)} %get-tuple-element.10.mass, bf16[48,216,216]{2,1,0:T(8,128)(2,1)S(1)} %get-tuple-element.11.jac, f32[2,512,128]{2,1,0:T(8,128)S(1)} %get-tuple-element.12.final, ...), custom_call_target="tpu_custom_call" | custom-call | tf_op jit(solution)/shard_map/place/pallas_call | solution.py:475

commit v4 on v3

--- a/solution.py
+++ b/solution.py
@@ -13,11 +13,18 @@
 REACH = 16
 LANES = 128
 SCHEDULE = (
-    ((0, 0, 3),),
-    ((0, 3, 5), (1, 0, 1)),
-    ((1, 1, 4),),
-    ((1, 5, 3),),
+    ((0, 0, 5),),
+    ((2, 0, 11),),
+    ((0, 5, 3), (1, 0, 8)),
+    (),
 )
+
+
+def overlap(first, size, other, length):
+    low, high = max(first, other), min(first + size, other + length)
+    return (low, high) if low < high else None
+
+
 SENDS = 8 + 2 * sum(len(part) for part in SCHEDULE)
 CLOSE = 2
 NT = (((1,), (1,)), ((), ()))
@@ -66,6 +73,8 @@
     share,
     first_layer,
     second_layer,
+    packed,
+    arrived,
     load_sem,
     tile_sem,
     send_sem,
@@ -159,22 +168,26 @@
 
     def tiles(phase):
         for which, start, size in SCHEDULE[phase]:
-            src, dst = ((mass_hbm, mass), (jac_hbm, jac))[which]
             slot = 8 + len(bulk)
-            bulk.append(
-                ToRight(
-                    slot,
-                    src.at[pl.ds(elems - MOVE + start, size)],
-                    dst.at[pl.ds(start, size)],
-                )
-            )
-            bulk.append(
-                ToLeft(
-                    slot + 1,
-                    src.at[pl.ds(start, size)],
-                    dst.at[pl.ds(MOVE + elems + start, size)],
-                )
-            )
+            if which == 2:
+                part = pl.ds(start, size)
+                ends = [(packed.at[side, part], arrived.at[side, part]) for side in range(2)]
+            else:
+                src, dst = ((mass_hbm, mass), (jac_hbm, jac))[which]
+                lanes = pl.ds(0, LANES)
+                ends = [
+                    (
+                        src.at[pl.ds(elems - MOVE + start, size), :, lanes],
+                        dst.at[pl.ds(start, size), :, lanes],
+                    ),
+                    (
+                        src.at[pl.ds(start, size), :, lanes],
+                        dst.at[pl.ds(MOVE + elems + start, size), :, lanes],
+                    ),
+                ]
+            copies = (ToRight(slot, *ends[0]), ToLeft(slot + 1, *ends[1]))
+            bulk.append((which, copies[0]))
+            bulk.append((which, copies[1]))
 
     tiles(0)
 
@@ -202,6 +215,36 @@
     variables = inner.shape[0]
     wide = group * SLOT
     tall = group * hid
+    rest = nodes - LANES
+    both = 2 * MOVE
+    count_packed = packed.shape[1]
+
+    def other_lanes(i, first):
+        array = mass if i < MOVE else jac
+        return array, first + i % MOVE
+
+    def pack(side, first):
+        for j in range(count_packed):
+            pieces = []
+            for i in range(both):
+                shared = overlap(j * LANES, LANES, i * rest, rest)
+                if shared:
+                    array, at = other_lanes(i, first)
+                    low, high = (lane - i * rest + LANES for lane in shared)
+                    pieces.append(array[at, :, low:high])
+            packed[side, j] = jnp.concatenate(pieces, axis=1)
+
+    def unpack(side, first):
+        for i in range(both):
+            pieces = []
+            for j in range(count_packed):
+                shared = overlap(i * rest, rest, j * LANES, LANES)
+                if shared:
+                    low, high = (lane - j * LANES for lane in shared)
+                    pieces.append(arrived[side, j, :, low:high])
+            array, at = other_lanes(i, first)
+            array[at, :, LANES:nodes] = jnp.concatenate(pieces, axis=1)
+
     def prepare():
         for copy in small[1:]:
             copy.wait()
@@ -281,6 +324,10 @@
             3 + 2 * sweep, spot.at[pl.ds(own + rows - halo, halo)], spot.at[pl.ds(0, halo)]
         )
 
+        if sweep == 0:
+            jac_load.wait()
+            pack(0, elems)
+            pack(1, MOVE)
         tiles(sweep + 1)
         if sweep == 0:
             prepare()
@@ -296,8 +343,6 @@
             return 0
 
         lax.fori_loop(0, rows // wide // CLOSE, close, 0)
-        if sweep == 0:
-            jac_load.wait()
 
         def transport(i, _):
             for k in range(unroll):
@@ -351,11 +396,18 @@
     leading = gone - from_left + MOVE
     line = iota(info.shape, 0)
     info[...] = jnp.where(line == 0, leading, filled)
-    for copy in last + bulk:
+    for which, copy in bulk:
+        if which == 2:
+            copy.wait()
+    unpack(0, 0)
+    unpack(1, MOVE + elems)
+    for copy in last + [copy for which, copy in bulk if which != 2]:
         copy.wait()
 
 
-def place_kernel(mass, jac, final, info, out_mass, out_jac, out_final, zeros, sem):
+def place_kernel(
+    mass, jac, final, info, out_mass, out_jac, out_final, zeros, planes, sem, planes_sem
+):
     leading = jnp.max(info[0:1, :]).astype(jnp.int32)
     filled = jnp.max(info[1:2, :]).astype(jnp.int32)
     slots = out_mass.shape[0]
@@ -396,10 +448,13 @@
     alive = iota((slots, LANES), 0) < filled
     for var in range(variables):
         at = pl.ds(leading * SLOT + var, slots, stride=SLOT)
-        out_final[var, :, 0:LANES] = jnp.where(alive, final[0, at, :], 0.0)
-        out_final[var, :, LANES:nodes] = jnp.where(alive, final[1, at, :], 0.0)[:, : nodes - LANES]
+        planes[var, :, 0:LANES] = jnp.where(alive, final[0, at, :], 0.0)
+        planes[var, :, LANES:nodes] = jnp.where(alive, final[1, at, :], 0.0)[:, : nodes - LANES]
+    states = pltpu.make_async_copy(planes, out_final, planes_sem)
+    states.start()
     for dst in (out_mass, out_jac):
         pltpu.make_async_copy(dst, dst, sem).wait()
+    states.wait()
 
 
 def shards(
@@ -420,6 +475,7 @@
     slots = elems + 2 * MOVE
     rows = elems * SLOT
     span = rows + 2 * REACH * SLOT
+    full = -(-2 * MOVE * (nodes - LANES) // LANES)
     operands = (
         jnp.transpose(elem_state, (1, 0, 2)),
         mass_inverse,
@@ -462,6 +518,8 @@
             pltpu.VMEM((rows, faces), F32),
             pltpu.VMEM((4 * hid, 4 * SLOT), BF16),
             pltpu.VMEM((4 * SLOT, 4 * hid), BF16),
+            pltpu.VMEM((2, full, nodes, LANES), BF16),
+            pltpu.VMEM((2, full, nodes, LANES), BF16),
             dma((7,)),
             dma((3,)),
             dma((SENDS,)),
@@ -480,8 +538,13 @@
             jax.ShapeDtypeStruct((variables, slots, nodes), F32),
         ),
         in_specs=[near_by] * 4,
-        out_specs=(anywhere, anywhere, near_by),
-        scratch_shapes=[pltpu.VMEM((8, nodes, nodes), BF16), dma],
+        out_specs=(anywhere,) * 3,
+        scratch_shapes=[
+            pltpu.VMEM((8, nodes, nodes), BF16),
+            pltpu.VMEM((variables, slots, nodes), F32),
+            dma,
+            dma,
+        ],
         compiler_params=pltpu.CompilerParams(vmem_limit_bytes=24 * 2**20),
         name="place",
     )(mass, jac, final, info)

time: 37.7 us -> 33.8 us (0.90)
  Pallas kernels: 37 us -> 33 us
    pallas_call x1, Pallas kernels: 32.2 us -> 28.9 us  [shards(): pl.pallas_call(functools.partial(sweep_kernel, count), out_shape=(pltpu.V...]
    pallas_call x1, Pallas kernels: 4.78 us -> 4.15 us  [shards(): pl.pallas_call(place_kernel, out_shape=(jax.ShapeDtypeStruct((slots, node...]
where the time goes in v4:
time: 33.8 us; the launch traced here: 33.7 us
  Pallas kernels  33 us (98%)
  between operations  0.64 us (2%)
    pallas_call x1, Pallas kernels, shards(): pl.pallas_call(functools.partial(sweep_kernel, count), out_shape=(pltpu.V...  28.9 us
    pallas_call x1, Pallas kernels, shards(): pl.pallas_call(place_kernel, out_shape=(jax.ShapeDtypeStruct((slots, node...  4.15 us

profile of v4, /device:TPU:24, one launch (start us, length us, event | category | flops | bytes accessed | tf_op | source)
XLA Modules:
  0.0 33.7 jit_solution(17829193805393450146)
XLA Ops:
  0.6 28.9 %sweeps.1 = (bf16[48,216,216]{2,1,0:T(8,128)(2,1)S(1)}, bf16[48,216,216]{2,1,0:T(8,128)(2,1)S(1)}, f32[2,512,128]{2,1,0:T(8,128)S(1)}, f32[8,128]{1,0:T(8,128)S(1)}) custom-call(bf16[5,32,216]{2,1,0:T(8,128)(2,1)} %bitcast.7, bf16[32,216,216]{2,1,0:T(8,128)(2,1)} %mass_hbm.1, bf16[32,216,216]{2,1,0:T(8,128)(2,1)} %jac_hbm.1, s32[1,32]{1,0:T(1,128)} %bitcast.11, ...), custom_call_target="tpu_custom_call" | custom-call | tf_op jit(solution)/shard_map/sweeps/pallas_call | solution.py:493
  29.5 4.1 %place.1 = (bf16[48,216,216]{2,1,0:T(8,128)(2,1)}, bf16[48,216,216]{2,1,0:T(8,128)(2,1)}, f32[5,48,216]{2,1,0:T(8,128)}) custom-call(bf16[48,216,216]{2,1,0:T(8,128)(2,1)S(1)} %get-tuple-element.10.mass, bf16[48,216,216]{2,1,0:T(8,128)(2,1)S(1)} %get-tuple-element.11.jac, f32[2,512,128]{2,1,0:T(8,128)S(1)} %get-tuple-element.12.final, ...), custom_call_target="tpu_custom_call" | custom-call | tf_op jit(solution)/shard_map/place/pallas_call | solution.py:533

commit v5 on v4

--- a/solution.py
+++ b/solution.py
@@ -75,6 +75,7 @@
     second_layer,
     packed,
     arrived,
+    edges,
     load_sem,
     tile_sem,
     send_sem,
@@ -85,9 +86,26 @@
     left = lax.rem(me + count - 1, count)
     elems, nodes = mass_hbm.shape[0], mass_hbm.shape[2]
     rows = elems * SLOT
-    edge = MOVE * SLOT
-    halo = REACH * SLOT
+    variables = state.shape[0]
+    halo = REACH * variables
     core = pl.ds(MOVE, elems)
+
+    has_left = me > 0
+    has_right = me < count - 1
+    barrier = pltpu.get_barrier_semaphore()
+
+    def greet(device):
+        pl.semaphore_signal(
+            barrier, inc=1, device_id=(device,), device_id_type=pl.DeviceIdType.MESH
+        )
+
+    @pl.when(has_left)
+    def _():
+        greet(me - 1)
+
+    @pl.when(has_right)
+    def _():
+        greet(me + 1)
 
     small = [
         pltpu.make_async_copy(src, dst, load_sem.at[i])
@@ -116,23 +134,6 @@
     for copy in small + mass_load + [jac_load]:
         copy.start()
 
-    has_left = me > 0
-    has_right = me < count - 1
-    barrier = pltpu.get_barrier_semaphore()
-
-    def greet(device):
-        pl.semaphore_signal(
-            barrier, inc=1, device_id=(device,), device_id_type=pl.DeviceIdType.MESH
-        )
-
-    @pl.when(has_left)
-    def _():
-        greet(me - 1)
-
-    @pl.when(has_right)
-    def _():
-        greet(me + 1)
-
     pl.semaphore_wait(barrier, has_left.astype(jnp.int32) + has_right.astype(jnp.int32))
 
     def sender(slot, src, dst, device):
@@ -163,7 +164,6 @@
             pl.when(has_left)(self.copy.wait_send)
             pl.when(has_right)(self.copy.wait_recv)
 
-    meta = [ToRight(0, owner_hbm, owners.at[1]), ToLeft(1, owner_hbm, owners.at[2])]
     bulk = []
 
     def tiles(phase):
@@ -190,6 +190,7 @@
             bulk.append((which, copies[1]))
 
     tiles(0)
+    meta = [ToRight(0, owner_hbm, owners.at[1]), ToLeft(1, owner_hbm, owners.at[2])]
 
     @pl.when(jnp.logical_not(has_left))
     def _():
@@ -212,7 +213,6 @@
 
     group = 4
     hid = inner.shape[1]
-    variables = inner.shape[0]
     wide = group * SLOT
     tall = group * hid
     rest = nodes - LANES
@@ -255,7 +255,13 @@
         faces = near.shape[0]
         near_rows = dot(spread, local, NT)
         lane_var = (iota((rows, faces), 0) % SLOT).astype(F32)
-        target[...] = near_rows * SLOT + lane_var
+        before = lane_var * REACH + near_rows
+        inside = (near_rows - REACH) * SLOT + lane_var + halo
+        after = before + (halo + rows - REACH - elems)
+        column = jnp.where(
+            near_rows < REACH, before, jnp.where(near_rows < REACH + elems, inside, after)
+        )
+        target[...] = jnp.where((near_rows < 0) | (lane_var >= variables), -1.0, column)
         share[...] = dot(spread, penalty[...], NT)
         orders = jnp.broadcast_to(order[...].astype(F32), (SLOT, elems)).astype(BF16)
         limit = dot(spread, orders, NT)[:, 0:1] + 1.0
@@ -295,6 +301,10 @@
     unroll = 4
     upper = iota((2 * SLOT, nodes), 0) < SLOT
     own = halo
+    reach = REACH * SLOT
+    goal = iota((halo, reach), 0)
+    taken = (goal % REACH) * SLOT + goal // REACH
+    slim = (taken == iota((halo, reach), 1)).astype(F32).astype(BF16)
 
     for sweep in range(SWEEPS):
         spot = weighted.at[sweep]
@@ -314,16 +324,13 @@
             return 0
 
         lax.fori_loop(0, pairs // unroll // 2, weigh, 0)
-        to_left = ToLeft(
-            2 + 2 * sweep, spot.at[pl.ds(own, halo)], spot.at[pl.ds(own + rows, halo)]
-        )
+        edges[2 * sweep] = dot(slim, spot[own : own + reach, :]).astype(BF16)
+        to_left = ToLeft(2 + 2 * sweep, edges.at[2 * sweep], spot.at[pl.ds(own + rows, halo)])
         if sweep == 0:
             mass_load[1].wait()
         lax.fori_loop(pairs // unroll // 2, pairs // unroll, weigh, 0)
-        to_right = ToRight(
-            3 + 2 * sweep, spot.at[pl.ds(own + rows - halo, halo)], spot.at[pl.ds(0, halo)]
-        )
-
+        edges[2 * sweep + 1] = dot(slim, spot[own + rows - reach : own + rows, :]).astype(BF16)
+        to_right = ToRight(3 + 2 * sweep, edges.at[2 * sweep + 1], spot.at[pl.ds(0, halo)])
         if sweep == 0:
             jac_load.wait()
             pack(0, elems)
@@ -362,24 +369,28 @@
 
         def finish(i, _):
             at = pl.ds(pl.multiple_of(i * block, block), block)
-            frm = pl.ds(pl.multiple_of(own + i * block, block), block)
+            frm = pl.ds(pl.multiple_of(own + i * block, 2 * SLOT), block)
             beside = dot(couple[0, at, :], spot[...]) + dot(couple[1, at, :], spot[...])
             total = jnp.sum(share[at, :], axis=1, keepdims=True)
             coupling = beside - total * spot[frm, :].astype(F32)
             value = (current[at, :] + added[at, :] + coupling) * keep[at, :]
             if sweep == SWEEPS - 1:
-                to = pl.ds(pl.multiple_of(edge + i * block, block), block)
-                final[0, to, :] = value[:, :LANES]
-                final[1, to, 0 : nodes - LANES] = value[:, LANES:]
+                many = block // SLOT
+                to = pl.ds(MOVE + i * many, many)
+                cut = value.reshape(many, SLOT, nodes)
+                final[0, to] = cut[:, :, :LANES]
+                final[1, to, :, 0 : nodes - LANES] = cut[:, :, LANES:]
             else:
                 current[at, :] = value
             return 0
 
         lax.fori_loop(0, rows // block, finish, 0)
 
+    used = pl.ds(0, variables)
+    beyond = pl.ds(MOVE + elems, MOVE)
     last = [
-        ToRight(6, final.at[:, pl.ds(rows, edge)], final.at[:, pl.ds(0, edge)]),
-        ToLeft(7, final.at[:, pl.ds(edge, edge)], final.at[:, pl.ds(edge + rows, edge)]),
+        ToRight(6, final.at[:, pl.ds(elems, MOVE), used], final.at[:, pl.ds(0, MOVE), used]),
+        ToLeft(7, final.at[:, pl.ds(MOVE, MOVE), used], final.at[:, beyond, used]),
     ]
     tiles(SWEEPS + 1)
     for copy in meta:
@@ -447,9 +458,9 @@
     nodes = out_final.shape[2]
     alive = iota((slots, LANES), 0) < filled
     for var in range(variables):
-        at = pl.ds(leading * SLOT + var, slots, stride=SLOT)
-        planes[var, :, 0:LANES] = jnp.where(alive, final[0, at, :], 0.0)
-        planes[var, :, LANES:nodes] = jnp.where(alive, final[1, at, :], 0.0)[:, : nodes - LANES]
+        at = pl.ds(leading, slots)
+        planes[var, :, 0:LANES] = jnp.where(alive, final[0, at, var, :], 0.0)
+        planes[var, :, LANES:nodes] = jnp.where(alive, final[1, at, var, :], 0.0)[:, : nodes - LANES]
     states = pltpu.make_async_copy(planes, out_final, planes_sem)
     states.start()
     for dst in (out_mass, out_jac):
@@ -474,7 +485,7 @@
     count = lax.axis_size("dom")
     slots = elems + 2 * MOVE
     rows = elems * SLOT
-    span = rows + 2 * REACH * SLOT
+    span = rows + 2 * REACH * variables
     full = -(-2 * MOVE * (nodes - LANES) // LANES)
     operands = (
         jnp.transpose(elem_state, (1, 0, 2)),
@@ -495,7 +506,7 @@
         out_shape=(
             pltpu.VMEM((slots, nodes, nodes), BF16),
             pltpu.VMEM((slots, nodes, nodes), BF16),
-            pltpu.VMEM((2, (slots + 2 * MOVE) * SLOT, LANES), F32),
+            pltpu.VMEM((2, slots + 2 * MOVE, SLOT, LANES), F32),
             pltpu.VMEM((8, 128), F32),
         ),
         in_specs=[anywhere] * 9,
@@ -520,6 +531,7 @@
             pltpu.VMEM((4 * SLOT, 4 * hid), BF16),
             pltpu.VMEM((2, full, nodes, LANES), BF16),
             pltpu.VMEM((2, full, nodes, LANES), BF16),
+            pltpu.VMEM((2 * SWEEPS, REACH * variables, nodes), BF16),
             dma((7,)),
             dma((3,)),
             dma((SENDS,)),

time: 33.8 us -> 33.2 us (0.982)
  Pallas kernels: 33 us -> 32.5 us
    pallas_call x1, Pallas kernels: 28.9 us -> 28.3 us  [shards(): pl.pallas_call(functools.partial(sweep_kernel, count), out_shape=(pltpu.V...]
where the time goes in v5:
time: 33.2 us; the launch traced here: 33.1 us
  Pallas kernels  32.5 us (98%)
  between operations  0.64 us (2%)
    pallas_call x1, Pallas kernels, shards(): pl.pallas_call(functools.partial(sweep_kernel, count), out_shape=(pltpu.V...  28.3 us
    pallas_call x1, Pallas kernels, shards(): pl.pallas_call(place_kernel, out_shape=(jax.ShapeDtypeStruct((slots, node...  4.15 us

profile of v5, /device:TPU:24, one launch (start us, length us, event | category | flops | bytes accessed | tf_op | source)
XLA Modules:
  0.0 33.1 jit_solution(6457257006989117974)
XLA Ops:
  0.6 28.3 %sweeps.1 = (bf16[48,216,216]{2,1,0:T(8,128)(2,1)S(1)}, bf16[48,216,216]{2,1,0:T(8,128)(2,1)S(1)}, f32[2,64,8,128]{3,2,1,0:T(8,128)S(1)}, f32[8,128]{1,0:T(8,128)S(1)}) custom-call(bf16[5,32,216]{2,1,0:T(8,128)(2,1)} %bitcast.7, bf16[32,216,216]{2,1,0:T(8,128)(2,1)} %mass_hbm.1, bf16[32,216,216]{2,1,0:T(8,128)(2,1)} %jac_hbm.1, s32[1,32]{1,0:T(1,128)} %bitcast.11, ...), custom_call_target="tpu_custom_call" | custom-call | tf_op jit(solution)/shard_map/sweeps/pallas_call | solution.py:504
  29.0 4.1 %place.1 = (bf16[48,216,216]{2,1,0:T(8,128)(2,1)}, bf16[48,216,216]{2,1,0:T(8,128)(2,1)}, f32[5,48,216]{2,1,0:T(8,128)}) custom-call(bf16[48,216,216]{2,1,0:T(8,128)(2,1)S(1)} %get-tuple-element.10.mass, bf16[48,216,216]{2,1,0:T(8,128)(2,1)S(1)} %get-tuple-element.11.jac, f32[2,64,8,128]{3,2,1,0:T(8,128)S(1)} %get-tuple-element.12.final, ...), custom_call_target="tpu_custom_call" | custom-call | tf_op jit(solution)/shard_map/place/pallas_call | solution.py:545
